TPU v7x, 32 devices: a whole 2x2x4 slice. The times are simulated.
32 devices in a mesh: fsdp: 8 (over z, y), dp: 4 (over x, core).
Axes of the slice: x: 2, y: 2, z: 4, core: 2. Of those that a mesh axis runs over, the one named last changes fastest.
Arguments:
- tokens: bfloat16 [24576, 576], P(('fsdp', 'dp')), may hold values from -6 to 6
- cotangent: bfloat16 [24576, 576], P(('fsdp', 'dp')), may hold values from -6 to 6
- lengths: int32 [8, 3], P('fsdp'), may hold values from 1 to 1536, 2304 in all within a row
- assignment: int32 [8, 24], P('fsdp'), may hold values from 0 to 23, as said below
- norm_gains: float32 [576, 2], P('fsdp'), may hold values from 0.5 to 1.5
- gain_momentum: float32 [576, 2], P('fsdp'), may hold values from -160 to 160
- w_query: float32 [576, 576], P('fsdp'), may hold values from -0.25 to 0.25
- w_keyval: float32 [576, 2, 192], P('fsdp'), may hold values from -0.25 to 0.25
- w_out: float32 [576, 576], P('fsdp'), may hold values from -1 to 1
- w_gateup: float32 [576, 2, 1536], P('fsdp'), may hold values from -0.25 to 0.25
- w_down: float32 [1536, 576], P('fsdp'), may hold values from -0.15625 to 0.15625
- m_query: float32 [576, 576], P('fsdp'), may hold values from -160 to 160
- m_keyval: float32 [576, 2, 192], P('fsdp'), may hold values from -160 to 160
- m_out: float32 [576, 576], P('fsdp'), may hold values from -160 to 160
- m_gateup: float32 [576, 2, 1536], P('fsdp'), may hold values from -160 to 160
- m_down: float32 [1536, 576], P('fsdp'), may hold values from -160 to 160
Outputs:
- activations: bfloat16 [24576, 576], P(('fsdp', 'dp'))
- input_grad: float32 [24576, 576], P(('fsdp', 'dp'))
- gain_grads: float32 [576, 2], P('fsdp')
- gain_moments: float32 [576, 2], P('fsdp')
- gain_values: float32 [576, 2], P('fsdp')
- query_grad: float32 [576, 576], P('fsdp')
- query_moment: float32 [576, 576], P('fsdp')
- query_new: float32 [576, 576], P('fsdp')
- keyval_grad: float32 [576, 2, 192], P('fsdp')
- keyval_moment: float32 [576, 2, 192], P('fsdp')
- keyval_new: float32 [576, 2, 192], P('fsdp')
- outproj_grad: float32 [576, 576], P('fsdp')
- outproj_moment: float32 [576, 576], P('fsdp')
- outproj_new: float32 [576, 576], P('fsdp')
- gateup_grad: float32 [576, 2, 1536], P('fsdp')
- gateup_moment: float32 [576, 2, 1536], P('fsdp')
- gateup_new: float32 [576, 2, 1536], P('fsdp')
- down_grad: float32 [1536, 576], P('fsdp')
- down_moment: float32 [1536, 576], P('fsdp')
- down_new: float32 [1536, 576], P('fsdp')
Inputs may be any that keep to these rules, and one draw needn't show every extreme that they name: Row g holds the lengths of the 3 sequences of group g in order; they sum to 2304. `assignment`: each row is a permutation of 0 to 23; entry b of row g places the group's b-th block in rows value * 128 to value * 128 + 127 of the group, held by the device at dp index value // 6.
All inputs are finite; a program needn't handle non-finite values.
Results may differ from a plain program's by a relative error of at most 0.023.
Values may be sent and summed in bfloat16 or wider, within the bound.
A program may use at most 192 MiB of HBM per device.

v0:
```python
from functools import partial
import math

import jax
import jax.numpy as jnp
from jax import lax
from jax.sharding import PartitionSpec as P

D = 576
HEADS = 9
KVH = 3
HD = 64
FF = 1536
BLK = 128
SEQS_G = 3
NS_STEPS = 5
QW = 576
KVW = 192


EPS = 1e-05
THETA = 100000.0
MOMENTUM_DECAY = 0.95
GAIN_DECAY = 0.9
MUON_RATE = 0.03
GAIN_SCALE = 0.4
COEF_A = 3.4445
COEF_B = -4.775
COEF_C = 2.0315
HIGHEST = lax.Precision.HIGHEST


def for_sending(value):
    return jax.tree.map(lambda a: a.astype(jnp.bfloat16) if a.dtype == jnp.float32 else a, value)


def group_meta(length_row, assign_row, block_count):
    slot_index = jnp.arange(block_count, dtype=jnp.int32)
    block_sizes = (length_row + BLK - 1) // BLK
    block_start = jnp.cumsum(block_sizes) - block_sizes
    block_of = jnp.sum(
        jnp.where(assign_row[:, None] == slot_index[None, :], slot_index[:, None], 0), axis=0
    )
    inside = (block_of[:, None] >= block_start[None, :]) & (
        block_of[:, None] < (block_start + block_sizes)[None, :]
    )
    seq_index = jnp.arange(SEQS_G, dtype=jnp.int32)
    seq_of = jnp.sum(jnp.where(inside, seq_index[None, :], 0), axis=1)
    first_block = jnp.sum(jnp.where(inside, block_start[None, :], 0), axis=1)
    seq_length = jnp.sum(jnp.where(inside, length_row[None, :], 0), axis=1)
    used = jnp.any(inside, axis=1)
    offset = (block_of - first_block)[:, None] * BLK + jnp.arange(BLK, dtype=jnp.int32)[None, :]
    living = used[:, None] & (offset < seq_length[:, None])
    row_index = jnp.arange(block_count * BLK, dtype=jnp.int32).reshape(block_count, BLK)
    seq_ids = jnp.where(living, seq_of[:, None], SEQS_G + row_index)
    positions = jnp.where(living, offset, 0)
    return (seq_ids.reshape(-1), positions.reshape(-1), living.reshape(-1))


def rope_tables(positions):
    freq = jnp.exp(jnp.arange(HD // 2, dtype=jnp.float32) * (-2.0 * math.log(THETA) / HD))
    angles = positions.astype(jnp.float32)[:, None] * freq[None, :]
    return (jnp.cos(angles), jnp.sin(angles))


def rotate(values, cosine, sine):
    half = HD // 2
    first = values[..., :half]
    second = values[..., half:]
    cos_part = cosine[:, None, :]
    sin_part = sine[:, None, :]
    return jnp.concatenate(
        [first * cos_part - second * sin_part, second * cos_part + first * sin_part], axis=-1
    )


def rotate_back(values, cosine, sine):
    half = HD // 2
    first = values[..., :half]
    second = values[..., half:]
    cos_part = cosine[:, None, :]
    sin_part = sine[:, None, :]
    return jnp.concatenate(
        [first * cos_part + second * sin_part, second * cos_part - first * sin_part], axis=-1
    )


def contract(left, right, left_dim, right_dim):
    return lax.dot_general(
        left, right, (((left_dim,), (right_dim,)), ((), ())), preferred_element_type=jnp.float32
    )


def orthogonal(matrix):
    flipped = matrix.shape[0] > matrix.shape[1]
    iterate = matrix.T if flipped else matrix
    iterate = iterate / (jnp.sqrt(jnp.sum(iterate * iterate)) + 1e-07)
    for turn in range(NS_STEPS):
        gram_matrix = jnp.dot(iterate, iterate.T, precision=HIGHEST)
        polynomial = COEF_B * gram_matrix + COEF_C * jnp.dot(
            gram_matrix, gram_matrix, precision=HIGHEST
        )
        iterate = COEF_A * iterate + jnp.dot(polynomial, iterate, precision=HIGHEST)
    return iterate.T if flipped else iterate


def muon_step(matrix):
    return MUON_RATE * math.sqrt(max(matrix.shape[0], matrix.shape[1])) * orthogonal(matrix)


def owner_branch(matrix_rows, matrix_cols, widest, received):
    group_size = received.shape[0]
    shard_size = matrix_rows * matrix_cols // group_size
    full_matrix = received[:, :shard_size].reshape(matrix_rows, matrix_cols)
    update_rows = muon_step(full_matrix).reshape(group_size, shard_size)
    return jnp.pad(update_rows, ((0, 0), (0, widest - shard_size)))


def zero_branch(received):
    return jnp.zeros_like(received)


def local(
    tokens,
    cotangent,
    lengths,
    assignment,
    norm_gains,
    gain_momentum,
    w_query,
    w_keyval,
    w_out,
    w_gateup,
    w_down,
    m_query,
    m_keyval,
    m_out,
    m_gateup,
    m_down,
):
    row_count = tokens.shape[0]
    fsdp_size = lax.axis_size("fsdp")
    fsdp_index = lax.axis_index("fsdp")
    block_count = assignment.shape[1]
    group_rows = block_count * BLK
    head_group = HEADS // KVH
    scale = 1.0 / math.sqrt(HD)
    gain_rate = GAIN_SCALE / math.sqrt(group_rows * 3 // 4 * fsdp_size)
    seq_all, pos_all, live_all = group_meta(lengths[0], assignment[0], block_count)
    start_row = lax.axis_index("dp") * row_count
    my_seq = lax.dynamic_slice_in_dim(seq_all, start_row, row_count)
    my_pos = lax.dynamic_slice_in_dim(pos_all, start_row, row_count)
    my_live = lax.dynamic_slice_in_dim(live_all.astype(jnp.float32), start_row, row_count)
    shard_low = (
        w_query.astype(jnp.bfloat16),
        w_keyval.astype(jnp.bfloat16),
        w_out.astype(jnp.bfloat16),
        w_gateup.astype(jnp.bfloat16),
        w_down.astype(jnp.bfloat16),
        norm_gains.astype(jnp.bfloat16),
    )
    weights = (
        lax.all_gather(shard_low[0], "fsdp", axis=0, tiled=True),
        lax.all_gather(shard_low[1], "fsdp", axis=0, tiled=True),
        lax.all_gather(shard_low[2], "fsdp", axis=0, tiled=True),
        lax.all_gather(shard_low[3], "fsdp", axis=0, tiled=True),
        lax.all_gather(shard_low[4], "fsdp", axis=0, tiled=True),
        lax.all_gather(shard_low[5], "fsdp", axis=0, tiled=True),
    )
    query_full, keyval_full, outproj_full, gateup_full, down_full, gains_full = weights
    gain_values = gains_full.astype(jnp.float32)
    inputs = tokens.astype(jnp.float32)
    inv_one = lax.rsqrt(jnp.mean(inputs * inputs, axis=-1, keepdims=True) + EPS)
    norm_one = inputs * inv_one
    normed = (norm_one * gain_values[:, 0]).astype(jnp.bfloat16)
    query_lin = jnp.dot(normed, query_full, preferred_element_type=jnp.float32)
    keyval_lin = jnp.dot(
        normed, keyval_full.reshape(D, 2 * KVW), preferred_element_type=jnp.float32
    )
    cosine, sine = rope_tables(my_pos)
    queries = (
        rotate(query_lin.reshape(row_count, HEADS, HD), cosine, sine)
        .astype(jnp.bfloat16)
        .reshape(row_count, KVH, head_group, HD)
    )
    key_rot = rotate(keyval_lin[:, :KVW].reshape(row_count, KVH, HD), cosine, sine).reshape(
        row_count, KVW
    )
    outgoing_kv = jnp.concatenate([key_rot, keyval_lin[:, KVW:]], axis=1).astype(jnp.bfloat16)
    group_kv = lax.all_gather(outgoing_kv, "dp", axis=0, tiled=True)
    key_rows = min(512, group_rows)
    key_blocks = group_rows // key_rows
    blocked = (
        group_kv.reshape(key_blocks, key_rows, 2, KVH, HD),
        seq_all.reshape(key_blocks, key_rows),
        pos_all.reshape(key_blocks, key_rows),
    )

    def block_scores(block_item):
        kv_block, seq_block, pos_block = block_item
        scores = (
            jnp.einsum(
                "rhjd,khd->hjrk", queries, kv_block[:, 0], preferred_element_type=jnp.float32
            )
            * scale
        )
        allowed = (seq_block[None, :] == my_seq[:, None]) & (pos_block[None, :] <= my_pos[:, None])
        return (jnp.where(allowed, scores, -1e30), allowed)

    def peak_step(carry, block_item):
        peak, running = carry
        masked, allowed = block_scores(block_item)
        new_peak = jnp.maximum(peak, jnp.max(masked, axis=-1))
        running = running * jnp.exp(peak - new_peak) + jnp.sum(
            jnp.where(allowed, jnp.exp(masked - new_peak[..., None]), 0.0), axis=-1
        )
        return ((new_peak, running), None)

    start_peak = jnp.full((KVH, head_group, row_count), -1e30, jnp.float32)
    (peak, running), unused = lax.scan(peak_step, (start_peak, jnp.zeros_like(start_peak)), blocked)
    log_total = peak + jnp.log(running)

    def probs_of(block_item):
        masked, allowed = block_scores(block_item)
        return jnp.where(allowed, jnp.exp(masked - log_total[..., None]), 0.0)

    def mix_step(accum, block_item):
        probs_low = probs_of(block_item).astype(jnp.bfloat16)
        return (
            accum
            + jnp.einsum(
                "hjrk,khd->rhjd", probs_low, block_item[0][:, 1], preferred_element_type=jnp.float32
            ),
            None,
        )

    attended_heads, unused = lax.scan(
        mix_step, jnp.zeros((row_count, KVH, head_group, HD), jnp.float32), blocked
    )
    attended_low = attended_heads.reshape(row_count, QW).astype(jnp.bfloat16)
    residual = inputs + jnp.dot(attended_low, outproj_full, preferred_element_type=jnp.float32)
    inv_two = lax.rsqrt(jnp.mean(residual * residual, axis=-1, keepdims=True) + EPS)
    norm_two = residual * inv_two
    second = (norm_two * gain_values[:, 1]).astype(jnp.bfloat16)
    gate_up = jnp.dot(second, gateup_full.reshape(D, 2 * FF), preferred_element_type=jnp.float32)
    gate_part = gate_up[:, :FF]
    up_part = gate_up[:, FF:]
    sigma = jax.nn.sigmoid(gate_part)
    swish = gate_part * sigma
    hidden = (swish * up_part).astype(jnp.bfloat16)
    activations = (
        residual + jnp.dot(hidden, down_full, preferred_element_type=jnp.float32)
    ).astype(jnp.bfloat16)
    back_weights = (
        lax.all_gather(shard_low[0], "fsdp", axis=0, tiled=True),
        lax.all_gather(shard_low[1], "fsdp", axis=0, tiled=True),
        lax.all_gather(shard_low[2], "fsdp", axis=0, tiled=True),
        lax.all_gather(shard_low[3], "fsdp", axis=0, tiled=True),
        lax.all_gather(shard_low[4], "fsdp", axis=0, tiled=True),
        lax.all_gather(shard_low[5], "fsdp", axis=0, tiled=True),
    )
    query_back, keyval_back, outproj_back, gateup_back, down_back = back_weights[:5]
    grad_final = cotangent.astype(jnp.float32) * my_live[:, None]
    grad_mlp = grad_final.astype(jnp.bfloat16)
    grad_down = contract(hidden, grad_mlp, 0, 0)
    grad_hidden = contract(grad_mlp, down_back, 1, 1)
    grad_gate = grad_hidden * up_part * sigma * (1.0 + gate_part * (1.0 - sigma))
    grad_gu = jnp.concatenate([grad_gate, grad_hidden * swish], axis=1).astype(jnp.bfloat16)
    grad_gateup = contract(second, grad_gu, 0, 0)
    grad_second = contract(grad_gu, gateup_back.reshape(D, 2 * FF), 1, 1)
    scaled_two = grad_second * gain_values[:, 1]
    grad_residual = grad_final + inv_two * (
        scaled_two - norm_two * jnp.mean(scaled_two * norm_two, axis=-1, keepdims=True)
    )
    grad_branch = grad_residual.astype(jnp.bfloat16)
    grad_outproj = contract(attended_low, grad_branch, 0, 0)
    grad_att = (
        contract(grad_branch, outproj_back, 1, 1)
        .astype(jnp.bfloat16)
        .reshape(row_count, KVH, head_group, HD)
    )
    delta = jnp.transpose(
        jnp.sum(grad_att.astype(jnp.float32) * attended_heads, axis=-1), (1, 2, 0)
    )

    def back_step(dq_accum, block_item):
        probs = probs_of(block_item)
        probs_low = probs.astype(jnp.bfloat16)
        key_part = block_item[0][:, 0]
        value_part = block_item[0][:, 1]
        value_grad = jnp.einsum(
            "hjrk,rhjd->khd", probs_low, grad_att, preferred_element_type=jnp.float32
        )
        prob_grad = jnp.einsum(
            "rhjd,khd->hjrk", grad_att, value_part, preferred_element_type=jnp.float32
        )
        score_grad = (probs * (prob_grad - delta[..., None])).astype(jnp.bfloat16)
        dq_accum = (
            dq_accum
            + jnp.einsum("hjrk,khd->rhjd", score_grad, key_part, preferred_element_type=jnp.float32)
            * scale
        )
        key_grad = (
            jnp.einsum("hjrk,rhjd->khd", score_grad, queries, preferred_element_type=jnp.float32)
            * scale
        )
        return (
            dq_accum,
            jnp.concatenate(
                [key_grad.reshape(key_rows, KVW), value_grad.reshape(key_rows, KVW)], axis=1
            ),
        )

    grad_qrot, kv_terms = lax.scan(
        back_step, jnp.zeros((row_count, KVH, head_group, HD), jnp.float32), blocked
    )
    kv_grad = lax.psum_scatter(
        kv_terms.reshape(group_rows, 2 * KVW).astype(jnp.bfloat16),
        "dp",
        scatter_dimension=0,
        tiled=True,
    ).astype(jnp.float32)
    grad_klin = rotate_back(kv_grad[:, :KVW].reshape(row_count, KVH, HD), cosine, sine).reshape(
        row_count, KVW
    )
    grad_kv = jnp.concatenate([grad_klin, kv_grad[:, KVW:]], axis=1).astype(jnp.bfloat16)
    grad_q = (
        rotate_back(grad_qrot.reshape(row_count, HEADS, HD), cosine, sine)
        .reshape(row_count, QW)
        .astype(jnp.bfloat16)
    )
    grad_query = contract(normed, grad_q, 0, 0)
    grad_keyval = contract(normed, grad_kv, 0, 0)
    grad_normed = contract(grad_q, query_back, 1, 1) + contract(
        grad_kv, keyval_back.reshape(D, 2 * KVW), 1, 1
    )
    scaled_one = grad_normed * gain_values[:, 0]
    input_grad = grad_residual + inv_one * (
        scaled_one - norm_one * jnp.mean(scaled_one * norm_one, axis=-1, keepdims=True)
    )
    grad_gains = jnp.stack(
        [jnp.sum(grad_normed * norm_one, axis=0), jnp.sum(grad_second * norm_two, axis=0)], axis=1
    )
    local_grads = (
        grad_query,
        grad_keyval.reshape(D, 2, KVW),
        grad_outproj,
        grad_gateup.reshape(D, 2, FF),
        grad_down,
        grad_gains,
    )
    owned = (
        lax.psum_scatter(
            local_grads[0].astype(jnp.bfloat16), "fsdp", scatter_dimension=0, tiled=True
        ).astype(jnp.float32),
        lax.psum_scatter(
            local_grads[1].astype(jnp.bfloat16), "fsdp", scatter_dimension=0, tiled=True
        ).astype(jnp.float32),
        lax.psum_scatter(
            local_grads[2].astype(jnp.bfloat16), "fsdp", scatter_dimension=0, tiled=True
        ).astype(jnp.float32),
        lax.psum_scatter(
            local_grads[3].astype(jnp.bfloat16), "fsdp", scatter_dimension=0, tiled=True
        ).astype(jnp.float32),
        lax.psum_scatter(
            local_grads[4].astype(jnp.bfloat16), "fsdp", scatter_dimension=0, tiled=True
        ).astype(jnp.float32),
        lax.psum_scatter(
            local_grads[5].astype(jnp.bfloat16), "fsdp", scatter_dimension=0, tiled=True
        ).astype(jnp.float32),
    )
    owned = (
        lax.psum(owned[0].astype(jnp.bfloat16), "dp").astype(jnp.float32),
        lax.psum(owned[1].astype(jnp.bfloat16), "dp").astype(jnp.float32),
        lax.psum(owned[2].astype(jnp.bfloat16), "dp").astype(jnp.float32),
        lax.psum(owned[3].astype(jnp.bfloat16), "dp").astype(jnp.float32),
        lax.psum(owned[4].astype(jnp.bfloat16), "dp").astype(jnp.float32),
        lax.psum(owned[5].astype(jnp.bfloat16), "dp").astype(jnp.float32),
    )
    shard_query, shard_keyval, shard_outproj, shard_gateup, shard_down, shard_gains = owned
    gain_moments = GAIN_DECAY * gain_momentum + shard_gains
    new_query = MOMENTUM_DECAY * m_query + shard_query
    new_keyval = MOMENTUM_DECAY * m_keyval + shard_keyval
    new_outproj = MOMENTUM_DECAY * m_out + shard_outproj
    new_gateup = MOMENTUM_DECAY * m_gateup + shard_gateup
    new_down = MOMENTUM_DECAY * m_down + shard_down
    pieces = [
        new_query,
        new_keyval[:, 0, :],
        new_keyval[:, 1, :],
        new_outproj,
        new_gateup[:, 0, :],
        new_gateup[:, 1, :],
        new_down,
    ]
    flat_sizes = [matrix_piece.size for matrix_piece in pieces]
    widest = max(flat_sizes)
    padded = [
        jnp.pad(matrix_piece.reshape(-1), (0, widest - matrix_piece.size))
        for matrix_piece in pieces
    ]
    outgoing = jnp.stack(padded + [jnp.zeros((widest,), jnp.float32)] * (fsdp_size - len(pieces)))
    received = lax.all_to_all(
        outgoing.astype(jnp.bfloat16), "fsdp", split_axis=0, concat_axis=0, tiled=True
    ).astype(outgoing.dtype)
    branches = [
        partial(owner_branch, matrix_piece.shape[0] * fsdp_size, matrix_piece.shape[1], widest)
        for matrix_piece in pieces
    ] + [zero_branch]
    update_rows = lax.switch(jnp.minimum(fsdp_index, len(pieces)), branches, received)
    returned = jax.tree.map(
        lambda part, own: part.astype(own.dtype),
        lax.all_to_all(for_sending(update_rows), "fsdp", split_axis=0, concat_axis=0, tiled=True),
        update_rows,
    )
    updates = [returned[m, : flat_sizes[m]].reshape(pieces[m].shape) for m in range(len(pieces))]
    return (
        activations,
        input_grad,
        shard_gains,
        gain_moments,
        norm_gains - gain_rate * gain_moments,
        shard_query,
        new_query,
        w_query - updates[0],
        shard_keyval,
        new_keyval,
        w_keyval - jnp.stack([updates[1], updates[2]], axis=1),
        shard_outproj,
        new_outproj,
        w_out - updates[3],
        shard_gateup,
        new_gateup,
        w_gateup - jnp.stack([updates[4], updates[5]], axis=1),
        shard_down,
        new_down,
        w_down - updates[6],
    )


def solution(mesh):
    placed = (
        P(("fsdp", "dp"), None),
        P(("fsdp", "dp"), None),
        P("fsdp", None),
        P("fsdp", None),
        P("fsdp", None),
        P("fsdp", None),
        P("fsdp", None),
        P("fsdp", None, None),
        P("fsdp", None),
        P("fsdp", None, None),
        P("fsdp", None),
        P("fsdp", None),
        P("fsdp", None, None),
        P("fsdp", None),
        P("fsdp", None, None),
        P("fsdp", None),
    )
    return jax.shard_map(
        local,
        mesh=mesh,
        in_specs=placed,
        out_specs=(
            P(("fsdp", "dp"), None),
            P(("fsdp", "dp"), None),
            P("fsdp", None),
            P("fsdp", None),
            P("fsdp", None),
            P("fsdp", None),
            P("fsdp", None),
            P("fsdp", None),
            P("fsdp", None, None),
            P("fsdp", None, None),
            P("fsdp", None, None),
            P("fsdp", None),
            P("fsdp", None),
            P("fsdp", None),
            P("fsdp", None, None),
            P("fsdp", None, None),
            P("fsdp", None, None),
            P("fsdp", None),
            P("fsdp", None),
            P("fsdp", None),
        ),
        check_vma=False,
    )
```

profile of v0, /device:TPU:0, one launch (start us, length us, event | category | flops | bytes accessed | tf_op | source)
XLA Modules:
  0.0 1332.2 jit_solution(9836449974785411095)
XLA Ops:
  8.0 22.1 %all-gather = bf16[8,72,2]{1,2,0:T(2,128)(2,1)S(1)} all-gather(bf16[1,72,2]{1,2,0:T(2,128)(2,1)S(1)} %convert_bitcast_fusion.1), channel_id=1, replica_groups=mesh['fsdp'=8,'dp'=4] {'fsdp'}, dimensions={0}, use_global_device_ids=true | all-gather | bytes 2592 | tf_op jit(solution)/shard_map/all_gather | solution.py:168
  32.7 31.8 %all_gather.27 = bf16[576,2,192]{2,1,0:T(2,128)(2,1)S(1)} all-gather(bf16[72,2,192]{2,1,0:T(2,128)(2,1)S(1)} %convert_element_type.227), channel_id=1, replica_groups=mesh['fsdp'=8,'dp'=4] {'fsdp'}, dimensions={0}, use_global_device_ids=true | all-gather | bytes 497664 | tf_op jit(solution)/shard_map/all_gather | solution.py:164
  72.1 34.4 %all_gather.30 = bf16[576,576]{1,0:T(8,128)(2,1)} all-gather(bf16[72,576]{1,0:T(8,128)(2,1)S(1)} %convert_element_type.232), channel_id=1, replica_groups=mesh['fsdp'=8,'dp'=4] {'fsdp'}, dimensions={0}, use_global_device_ids=true | all-gather | bytes 746496 | tf_op jit(solution)/shard_map/all_gather | solution.py:165
  106.6 33.8 %all_gather.29 = bf16[576,576]{1,0:T(8,128)(2,1)S(1)} all-gather(bf16[72,576]{1,0:T(8,128)(2,1)S(1)} %convert_element_type.229), channel_id=1, replica_groups=mesh['fsdp'=8,'dp'=4] {'fsdp'}, dimensions={0}, use_global_device_ids=true | all-gather | bytes 746496 | tf_op jit(solution)/shard_map/all_gather | solution.py:163
  152.1 104.0 %while.37 = (s32[]{:T(128)}, f32[3,3,768]{2,1,0:T(4,128)S(1)}, f32[3,3,768]{2,1,0:T(4,128)S(1)}, s32[6,512]{1,0:T(8,128)S(1)}, s32[768]{0:T(1024)S(1)}, /*index=...) while((s32[]{:T(128)}, f32[3,3,768]{2,1,0:T(4,128)S(1)}, ...), condition=%wide.region_10.11_spmd.clone, body=%wide.region_7.10_spmd.clone.sunk | while | flops 482510592 | bytes 31736964 | solution.py:220
  160.9 8.4 select_reduce_fusion.6
  178.2 8.5 select_reduce_fusion.6
  195.6 8.5 select_reduce_fusion.6
  213.0 8.4 select_reduce_fusion.6
  256.1 53.5 %while.38 = (s32[]{:T(128)}, f32[768,3,3,64]{0,3,2,1:T(8,128)}, bf16[6,512,2,3,64]{1,4,3,2,0:T(8,128)(2,1)}, s32[6,512]{1,0:T(8,128)S(1)}, s32[768]{0:T(1024)S(1...) while((s32[]{:T(128)}, f32[768,3,3,64]{0,3,2,1:T(8,128)}, ...), condition=%wide.region_12.13_spmd.clone, body=%wide.region_11.12_spmd.clone.sunk | while | flops 925728768 | bytes 6435975 | solution.py:237
  325.4 10.0 multiply_convert_fusion.1
  344.2 182.6 %while.39 = (s32[]{:T(128)}, f32[768,3,3,64]{0,3,2,1:T(8,128)S(1)}, bf16[6,512,384]{2,1,0:T(8,128)(2,1)}, bf16[6,512,2,3,64]{1,4,3,2,0:T(8,128)(2,1)}, s32[6,512...) while((s32[]{:T(128)}, f32[768,3,3,64]{0,3,2,1:T(8,128)S(1)}, ...), condition=%wide.region_17.18_spmd.clone, body=%wide.region_16.17_spmd.clone.sunk | while | flops 2310881280 | bytes 76198040 | solution.py:314
  352.9 8.8 fusion.603
  383.3 8.8 fusion.603
  413.7 8.8 fusion.603
  444.2 8.8 fusion.603
  474.6 8.8 fusion.603
  504.9 8.8 fusion.603
  540.2 9.1 convert_element_type.256
  549.3 12.3 reduce-scatter.10.cloned.1.call-done
  586.8 23.0 %all-reduce.8 = bf16[576,2]{0,1:T(2,128)(2,1)S(1)} all-reduce(bf16[576,2]{0,1:T(2,128)(2,1)S(1)} %pad_maximum_fusion.11), channel_id=3, replica_groups=mesh['fsdp'=8,'dp'=4] {'fsdp'}, use_global_device_ids=true, to_apply=%region_22.23.clone | all-reduce | flops 1152 | bytes 4608
  609.9 111.8 %all-reduce.19.cloned.1.call-done = (bf16[576,2,192]{2,1,0:T(2,128)(2,1)}, bf16[576,2,1536]{2,1,0:T(2,128)(2,1)}) async-done(((bf16[576,2,192]{2,1,0:T(2,128)(2,1)}, bf16[576,2,1536]{2,1,0:T(2,128)(2,1)}), (bf16[576,2,192]{2,1,0:T(2,128)(2,1)}, bf16[576,2,1536]{2,1,0:T(2,128)(2,1)})) %all-reduce.19.cloned.1.call-update) | async-done | bytes 3981328
  723.8 61.6 %reduce-scatter.16.cloned.1.call-done = bf16[72,576]{1,0:T(8,128)(2,1)} async-done(((bf16[576,576]{1,0:T(8,128)(2,1)}), bf16[72,576]{1,0:T(8,128)(2,1)}) %reduce-scatter.16.cloned.1.call-update) | async-done | bytes 82960
  785.4 63.8 %reduce-scatter.14.cloned.1.call-done = bf16[72,576]{1,0:T(8,128)(2,1)} async-done(((bf16[576,576]{1,0:T(8,128)(2,1)}), bf16[72,576]{1,0:T(8,128)(2,1)}) %reduce-scatter.14.cloned.1.call-update) | async-done | bytes 82960
  849.2 69.7 %reduce-scatter.12.cloned.1.call-done = bf16[192,576]{1,0:T(8,128)(2,1)} async-done(((bf16[1536,576]{1,0:T(8,128)(2,1)}), bf16[192,576]{1,0:T(8,128)(2,1)}) %reduce-scatter.12.cloned.1.call-update) | async-done | bytes 221200 | tf_op jit(solution)/shard_map/reduce_scatter | solution.py:365
  919.9 12.6 all-reduce.14
  934.0 22.6 %all-reduce.21.cloned.1.call-done = (bf16[72,576]{1,0:T(8,128)(2,1)}, bf16[72,576]{1,0:T(8,128)(2,1)}, bf16[72,2,1536]{2,1,0:T(2,128)(2,1)}, bf16[192,576]{1,0:T(8,128)(2,1)}) async-done(((bf16[72,576]{1,0:T(8,128)(2,1)}, bf16[72,576]{1,0:T(8,128)(2,1)}, bf16[72,2,1536]{2,1,0:T(2,128)(2,1)}, bf16[192,576]{1,0:T(8,128)(2,1)}), (bf16[72,576]{1,0:T(8,128)(2,1)}, bf16[72,576]{1,0:T(8,128)(2,1)}, ...) | async-done | bytes 829456 | tf_op jit(solution)/shard_map/psum | solution.py:373
  973.8 38.1 %reduce.32 = bf16[8,110592]{1,0:T(8,128)(2,1)S(1)} reduce(bf16[8,1,110592]{2,1,0:T(2,128)(2,1)} %broadcast_dynamic-update-slice_fusion, bf16[]{:T(256)} %broadcast.857), dimensions={1}, to_apply=%broadcast_dynamic-update-slice_fusion.reduce_sub_computation | reduce | bytes 3538946 | tf_op jit(solution)/shard_map/stack | solution.py:402
  1020.2 40.6 %all-to-all-done = bf16[8,2,55296]{2,1,0:T(2,128)(2,1)} async-done(((bf16[8,2,55296]{2,1,0:T(2,128)(2,1)}), bf16[8,2,55296]{2,1,0:T(2,128)(2,1)}, u32[]{:S(2)}, u32[]{:S(2)}) %all-to-all-start) | async-done | bytes 1769504 | tf_op jit(solution)/shard_map/all_to_all | solution.py:403
  1065.6 111.9 %conditional.1 = (bf16[8,110592]{1,0:T(8,128)(2,1)}) conditional(s32[]{:T(128)} %clamp.3, bf16[8,1,110592]{2,1,0:T(2,128)(2,1)S(1)} %reshape.628, bf16[8,1,110592]{2,1,0:T(2,128)(2,1)S(1)} %reshape.628, bf16[8,1,110592]{2,1,0:T(2,128)(2,1)S(1)} %reshape.628, bf16[8,1,110592]{2,1,0:T(2,128)(2,1)S(1)} %reshape.628, ...), branch_computations={%region_34.36_spmd, %region_36.38_spmd, %region_38.40_spmd, %regio... | conditional | flops 72656846848 | bytes 229589120 | solution.py:410
  1183.8 79.8 %all-to-all-start.1 = ((bf16[8,2,55296]{2,1,0:T(2,128)(2,1)}), bf16[8,2,55296]{2,1,0:T(2,128)(2,1)}, u32[]{:S(2)}, u32[]{:S(2)}) async-start(bf16[8,2,55296]{2,1,0:T(2,128)(2,1)} %reshape.629), calls=%async_computation.3 | async-start | bytes 3538944 | tf_op jit(solution)/shard_map/all_to_all | solution.py:413
  1270.9 34.2 %all-to-all-done.1 = bf16[8,2,55296]{2,1,0:T(2,128)(2,1)} async-done(((bf16[8,2,55296]{2,1,0:T(2,128)(2,1)}), bf16[8,2,55296]{2,1,0:T(2,128)(2,1)}, u32[]{:S(2)}, u32[]{:S(2)}) %all-to-all-start.1) | async-done | bytes 1769504 | tf_op jit(solution)/shard_map/all_to_all | solution.py:413
  (445 shorter events, 477.4 us)
Async XLA Ops:
  7.2 58.3 %copy-start.9 = (bf16[768,576]{0,1:T(8,128)(2,1)S(1)}, bf16[768,576]{0,1:T(8,128)(2,1)}, u32[]{:S(2)}) copy-start(bf16[768,576]{0,1:T(8,128)(2,1)} %param.30) | copy-start | bytes 2654212
  7.2 134.8 %all-gather.5.cloned.1.call-start = ((), (), s32[]{:S(2)}) async-start(), calls=%async_computation.6 | async-start | bytes 2949120 | tf_op jit(solution)/shard_map/all_gather | solution.py:190
  30.3 110.1 %copy-start.57 = (f32[576]{0:T(1024)}, f32[576]{0:T(1024)S(1)}, u32[]{:S(2)}) copy-start(f32[576]{0:T(1024)S(1)} %get-tuple-element.653) | copy-start | bytes 6916
  31.7 108.7 %copy-start.60 = (f32[768]{0:T(1024)}, f32[768]{0:T(1024)S(1)}, u32[]{:S(2)}) copy-start(f32[768]{0:T(1024)S(1)} %add_rsqrt_fusion.1) | copy-start | bytes 9220
  68.1 73.3 %copy-start.29 = (f32[768,32]{0,1:T(8,128)}, f32[768,32]{0,1:T(8,128)S(1)}, u32[]{:S(2)}) copy-start(f32[768,32]{0,1:T(8,128)S(1)} %get-tuple-element.786) | copy-start | bytes 294916
  68.1 73.3 %copy-start.31 = (f32[768,32]{0,1:T(8,128)}, f32[768,32]{0,1:T(8,128)S(1)}, u32[]{:S(2)}) copy-start(f32[768,32]{0,1:T(8,128)S(1)} %get-tuple-element.787) | copy-start | bytes 294916
  69.2 244.6 %all-gather.7.cloned.1.call-start = ((), (), s32[]{:S(2)}) async-start(), calls=%async_computation.7 | async-start | bytes 3981312 | tf_op jit(solution)/shard_map/all_gather | solution.py:166
  70.7 254.7 %all-gather.9.cloned.1.call-start = ((), (), s32[]{:S(2)}) async-start(), calls=%async_computation.8 | async-start | bytes 2211840 | tf_op jit(solution)/shard_map/all_gather | solution.py:167
  71.5 490.2 %reduce-scatter.10.cloned.1.call-start = ((), (), s32[]{:S(2)}) async-start(), calls=%async_computation.9 | async-start | bytes 2949120 | tf_op jit(solution)/shard_map/reduce_scatter | solution.py:317
  71.8 267.3 %copy-start.64 = (f32[768]{0:T(1024)}, f32[768]{0:T(1024)S(1)}, u32[]{:S(2)}) copy-start(f32[768]{0:T(1024)S(1)} %dynamic-slice_convert_fusion) | copy-start | bytes 9220
  325.3 10.0 copy-start.6
  325.4 10.0 copy-start.17
  531.2 190.5 %all-reduce.19.cloned.1.call-start = ((), (), s32[]{:S(2)}) async-start(), calls=%async_computation.13 | async-start | bytes 8257536
  549.3 13.5 %copy-start.30 = (f32[768,32]{0,1:T(8,128)S(1)}, f32[768,32]{0,1:T(8,128)}, u32[]{:S(2)}) copy-start(f32[768,32]{0,1:T(8,128)} %copy-done.29) | copy-start | bytes 294916
  549.3 13.5 %copy-start.32 = (f32[768,32]{0,1:T(8,128)S(1)}, f32[768,32]{0,1:T(8,128)}, u32[]{:S(2)}) copy-start(f32[768,32]{0,1:T(8,128)} %copy-done.31) | copy-start | bytes 294916
  566.5 218.9 %reduce-scatter.16.cloned.1.call-start = ((), (), s32[]{:S(2)}) async-start(), calls=%async_computation.12 | async-start | bytes 829440
  570.9 278.3 %reduce-scatter.14.cloned.1.call-start = ((), (), s32[]{:S(2)}) async-start(), calls=%async_computation.11 | async-start | bytes 829440
  575.2 343.7 %reduce-scatter.12.cloned.1.call-start = ((), (), s32[]{:S(2)}) async-start(), calls=%async_computation.10 | async-start | bytes 2211840 | tf_op jit(solution)/shard_map/reduce_scatter | solution.py:365
  580.3 376.3 %all-reduce.21.cloned.1.call-start = ((), (), s32[]{:S(2)}) async-start(), calls=%async_computation.14 | async-start | bytes 1744896 | tf_op jit(solution)/shard_map/psum | solution.py:373
  586.8 345.8 %copy-start.56 = (f32[72,2,192]{2,1,0:T(2,128)S(1)}, f32[72,2,192]{2,1,0:T(2,128)}, u32[]{:S(2)}) copy-start(f32[72,2,192]{2,1,0:T(2,128)} %param.42) | copy-start | bytes 331780
  721.7 234.9 %copy-start.54 = (f32[72,576]{1,0:T(8,128)S(1)}, f32[72,576]{1,0:T(8,128)}, u32[]{:S(2)}) copy-start(f32[72,576]{1,0:T(8,128)} %param.41) | copy-start | bytes 497668
  919.0 39.5 %copy-start.55 = (f32[72,576]{1,0:T(8,128)S(1)}, f32[72,576]{1,0:T(8,128)}, u32[]{:S(2)}) copy-start(f32[72,576]{1,0:T(8,128)} %param.43) | copy-start | bytes 497668
  933.7 26.7 %copy-start.51 = (f32[192,576]{1,0:T(8,128)S(1)}, f32[192,576]{1,0:T(8,128)}, u32[]{:S(2)}) copy-start(f32[192,576]{1,0:T(8,128)} %param.45) | copy-start | bytes 1327108
  1014.7 46.1 %all-to-all-start = ((bf16[8,2,55296]{2,1,0:T(2,128)(2,1)}), bf16[8,2,55296]{2,1,0:T(2,128)(2,1)}, u32[]{:S(2)}, u32[]{:S(2)}) async-start(bf16[8,2,55296]{2,1,0:T(2,128)(2,1)} %reshape.627), calls=%async_computation.2 | async-start | bytes 3538944 | tf_op jit(solution)/shard_map/all_to_all | solution.py:403
  1183.8 79.8 %copy-start.19 = (f32[768,576]{0,1:T(8,128)S(1)}, f32[768,576]{0,1:T(8,128)}, u32[]{:S(2)}) copy-start(f32[768,576]{0,1:T(8,128)} %get-tuple-element.790) | copy-start | bytes 5308420
  1183.8 121.3 %all-to-all-start.1 = ((bf16[8,2,55296]{2,1,0:T(2,128)(2,1)}), bf16[8,2,55296]{2,1,0:T(2,128)(2,1)}, u32[]{:S(2)}, u32[]{:S(2)}) async-start(bf16[8,2,55296]{2,1,0:T(2,128)(2,1)} %reshape.629), calls=%async_computation.3 | async-start | bytes 3538944 | tf_op jit(solution)/shard_map/all_to_all | solution.py:413
  1263.6 5.0 copy-start.63
  1263.6 5.0 copy-start.3
  1263.6 5.0 copy-start.13
  1263.6 5.0 copy-start.14
  1263.6 5.0 copy-start.59
  1263.7 5.0 copy-start.62
  (47 other events, 93.6 us)
Sparse Core Ops, SparseCore 0:
  69.3 21.3 all-gather.4
  93.4 69.6 all-gather.6
  165.8 46.9 all-gather.8
  531.3 30.3 reduce-scatter.9
  566.6 155.0 all-reduce.18
  725.8 59.5 reduce-scatter.15
  789.7 59.4 reduce-scatter.13
  853.1 65.7 reduce-scatter.11
  922.1 34.4 all-reduce.20
where the time goes:
time: 1340 us; the launch traced here: 1330 us
  waiting for transfers between devices  417 us (31%)
  matrix products  374 us (28%)
  blocking collectives  158 us (12%)
  other arithmetic  132 us (10%)
  local copies, waits for them, and re-layouts  108 us (8%)
  starting transfers between devices  85.9 us (6%)
  loops' own time  40.6 us (3%)
  between operations  15.8 us (1%)
    unnamed x12, waiting for transfers between devices  237 us
    dot_general x12, matrix products, block_scores(): jnp.einsum('rhjd,khd->hjrk', queries, kv_block[:, 0], preferred_element_t...  86.4 us
    all_to_all x1, starting transfers between devices, local(): lax.all_to_all(for_sending(update_rows), 'fsdp', split_axis=0, concat_axi...  79.8 us
    reduce_scatter x1, waiting for transfers between devices, local(): lax.psum_scatter(local_grads[4].astype(jnp.bfloat16), 'fsdp', scatter_dim...  69.7 us
    dot_general x6, matrix products, back_step(): jnp.einsum('hjrk,rhjd->khd', probs_low, grad_att, preferred_element_type=...  53.1 us
    reduce_sum x6, other arithmetic, peak_step(): jnp.sum(jnp.where(allowed, jnp.exp(masked - new_peak[..., None]), 0.0), a...  50.7 us
    dot_general x6, matrix products, back_step(): jnp.einsum('rhjd,khd->hjrk', grad_att, value_part, preferred_element_type...  49.9 us
    unnamed x156, local copies, waits for them, and re-layouts  46.3 us
  transfers between devices with their start and end apart: 11, of which 8 were waited for; matrix products, arithmetic and copies ran while one was open for 17% of the time, Pallas kernels for 0%

commit v1 on v0

v1 whole, which is shorter than its diff:
```python
from functools import partial
import math

import jax
import jax.numpy as jnp
import numpy as np
from jax import lax
from jax.experimental import pallas as pl
from jax.experimental.pallas import tpu as pltpu
from jax.sharding import PartitionSpec as P

D = 576
HEADS = 9
KVH = 3
HD = 64
FF = 1536
BLK = 128
SEQS_G = 3
NS_STEPS = 5
QW = 576
KVW = 192
LONGEST = 12

EPS = 1e-05
THETA = 100000.0
MOMENTUM_DECAY = 0.95
GAIN_DECAY = 0.9
MUON_RATE = 0.03
GAIN_SCALE = 0.4
COEF_A = 3.4445
COEF_B = -4.775
COEF_C = 2.0315
SCALE = 1.0 / math.sqrt(HD)
HALF = 768
WIDE_A = 2 * (HALF + 128)
O_AT = HALF + 128
STEP = 256
F32, BF16 = jnp.float32, jnp.bfloat16


def vmem(count=1):
    return [pl.BlockSpec(memory_space=pltpu.VMEM)] * count


def dot(a, b):
    return lax.dot_general(a, b, (((1,), (0,)), ((), ())), preferred_element_type=F32)


def dot_nt(a, b):
    return lax.dot_general(a, b, (((1,), (1,)), ((), ())), preferred_element_type=F32)


def dot_tn(a, b):
    return lax.dot_general(a, b, (((0,), (0,)), ((), ())), preferred_element_type=F32)


def block_meta(length_row, assign_row, first_slot, slots):
    entries = jnp.arange(assign_row.shape[0], dtype=jnp.int32)
    sizes = (length_row + BLK - 1) // BLK
    start = jnp.cumsum(sizes) - sizes
    mine = first_slot + jnp.arange(slots, dtype=jnp.int32)
    entry = jnp.sum(jnp.where(assign_row[None, :] == mine[:, None], entries[None, :], 0), axis=1)
    inside = (entry[:, None] >= start[None, :]) & (entry[:, None] < (start + sizes)[None, :])
    first = jnp.sum(jnp.where(inside, start[None, :], 0), axis=1)
    size = jnp.sum(jnp.where(inside, length_row[None, :], 0), axis=1)
    used = jnp.any(inside, axis=1)
    place = jnp.where(used, entry - first, 0)
    live = jnp.where(used, jnp.clip(size - place * BLK, 0, BLK), 0)
    step = jnp.arange(LONGEST, dtype=jnp.int32)
    want = first[:, None] + step[None, :]
    keys = jnp.sum(
        jnp.where(want[:, :, None] == entries[None, None, :], assign_row[None, None, :], 0), axis=2
    )
    keys = jnp.where(used[:, None] & (step[None, :] <= place[:, None]), keys, mine[:, None])
    return jnp.concatenate(
        [place[:, None], live[:, None], (place // 2 + 1)[:, None], live[:, None], keys], axis=1
    )


def rope_constants():
    freq = np.exp(np.arange(HD // 2, dtype=np.float64) * (-2.0 * math.log(THETA) / HD))
    lanes = np.tile(freq, 4)
    inner = np.arange(BLK)[:, None] * lanes[None, :]
    outer = BLK * np.arange(16)[:, None] * lanes[None, :]
    return (
        np.stack([np.cos(inner), np.sin(inner)]).astype(np.float32),
        np.stack([np.cos(outer), np.sin(outer)]).astype(np.float32),
    )


def lane_index(rows):
    return lax.broadcasted_iota(jnp.int32, (rows, 128), 1)


def rope_tables(meta, slot, inner_ref, outer_ref):
    place, live = meta[slot, 0], meta[slot, 1]
    co, so = outer_ref[0, pl.ds(place, 1), :], outer_ref[1, pl.ds(place, 1), :]
    ci, si = inner_ref[0], inner_ref[1]
    lane = lane_index(BLK)
    row = lax.broadcasted_iota(jnp.int32, (BLK, 128), 0)
    turned = (row < live) & (lane < HD)
    cosine = jnp.where(turned, co * ci - so * si, 1.0)
    sine = jnp.where(turned, so * ci + co * si, 0.0)
    return cosine, jnp.where(lane < HD // 2, sine, 0.0), jnp.where(lane < HD // 2, 0.0, sine)


def rope(tile, tables):
    cosine, sine_low, sine_high = tables
    return (
        tile * cosine - pltpu.roll(tile, 128 - HD // 2, 1) * sine_low
        + pltpu.roll(tile, HD // 2, 1) * sine_high
    )


def rope_back(tile, tables):
    cosine, sine_low, sine_high = tables
    return (
        tile * cosine + pltpu.roll(tile, 128 - HD // 2, 1) * sine_low
        - pltpu.roll(tile, HD // 2, 1) * sine_high
    )


def swap(tile):
    return pltpu.roll(tile, HD, 1)


def gain_row(packed_ref, at):
    return packed_ref[:, at : at + 128].astype(F32).T[0:1, :]


def project_kernel(meta, x_ref, wa_ref, inner_ref, outer_ref, q_ref, kv_ref):
    gain = gain_row(wa_ref, HALF)
    low_lane = lane_index(BLK) < HD

    @pl.loop(0, x_ref.shape[0] // STEP)
    def _(i):
        x = x_ref[pl.ds(pl.multiple_of(i * STEP, STEP), STEP), :].astype(F32)
        inv = lax.rsqrt(jnp.mean(x * x, axis=1, keepdims=True) + EPS)
        normed = (x * inv * gain).astype(BF16)
        qk = dot(normed, wa_ref[:, :HALF])
        ov = dot(normed, wa_ref[:, O_AT + 512 : O_AT + HALF])
        for b in range(STEP // BLK):
            tables = rope_tables(meta, i * (STEP // BLK) + b, inner_ref, outer_ref)
            rows = pl.ds(pl.multiple_of(i * STEP + b * BLK, BLK), BLK)
            part = slice(b * BLK, (b + 1) * BLK)
            tiles = [qk[part, 128 * t : 128 * t + 128] for t in range(6)]
            for head in range(HEADS):
                tile = tiles[head // 2]
                tile = jnp.where(low_lane, swap(tile) if head % 2 else tile, 0.0)
                q_ref[rows, 128 * head : 128 * head + 128] = (rope(tile, tables) * SCALE).astype(BF16)
            values = [ov[part, :128], ov[part, 128:]]
            pairs = (
                (swap(tiles[4]), values[0]),
                (tiles[5], swap(values[1])),
                (swap(tiles[5]), values[1]),
            )
            for h in range(KVH):
                tile = jnp.where(low_lane, *pairs[h])
                kv_ref[rows, 128 * h : 128 * h + 128] = rope(tile, tables).astype(BF16)


def project(meta, tokens, packed, inner, outer):
    rows = tokens.shape[0]
    return pl.pallas_call(
        project_kernel,
        out_shape=(
            jax.ShapeDtypeStruct((rows, 128 * HEADS), BF16),
            jax.ShapeDtypeStruct((rows, 2 * KVW), BF16),
        ),
        in_specs=[pl.BlockSpec(memory_space=pltpu.SMEM)] + vmem(4),
        out_specs=tuple(vmem(2)),
        compiler_params=pltpu.CompilerParams(vmem_limit_bytes=48 << 20),
        name="project",
    )(meta, tokens, packed, inner, outer)


def chunk_bias(meta, slot, chunk):
    row = lax.broadcasted_iota(jnp.int32, (BLK, 2 * BLK), 0) + meta[slot, 0] * BLK
    column = lax.broadcasted_iota(jnp.int32, (BLK, 2 * BLK), 1) + chunk * (2 * BLK)
    live_end = meta[slot, 0] * BLK + meta[slot, 1]
    allowed = (column <= row) & ((row < live_end) | (column == row))
    bias = jnp.where(allowed, 0.0, -1e30)
    return jnp.concatenate([bias] * (HEADS // KVH), axis=0)


def key_tile(kv_ref, meta, slot, chunk, h):
    lanes = slice(128 * h, 128 * h + 128)
    one = pl.ds(pl.multiple_of(meta[slot, 4 + 2 * chunk] * BLK, BLK), BLK)
    two = pl.ds(pl.multiple_of(meta[slot, 5 + 2 * chunk] * BLK, BLK), BLK)
    return jnp.concatenate([kv_ref[one, lanes], kv_ref[two, lanes]], axis=0)


def stacked(ref, rows, h):
    at = 128 * (HEADS // KVH) * h
    return jnp.concatenate(
        [ref[rows, at + 128 * j : at + 128 * j + 128] for j in range(HEADS // KVH)], axis=0
    )


def twice(value):
    return jnp.concatenate([value, value], axis=1)


def attention_forward(meta, q_ref, kv_ref, mixed_s, low_s, lse_s, peak_s, accum_s):
    group = HEADS // KVH
    low_lane = lane_index(group * BLK) < HD
    low_key = lane_index(2 * BLK) < HD

    @pl.loop(0, q_ref.shape[0] // BLK)
    def _(slot):
        rows = pl.ds(pl.multiple_of(slot * BLK, BLK), BLK)
        peak_s[...] = jnp.full_like(peak_s, -1e30)
        accum_s[...] = jnp.zeros_like(accum_s)

        @pl.loop(0, meta[slot, 2])
        def _(chunk):
            bias = chunk_bias(meta, slot, chunk)
            for h in range(KVH):
                tile = key_tile(kv_ref, meta, slot, chunk, h)
                scores = dot_nt(stacked(q_ref, rows, h), tile) + bias
                old = peak_s[h]
                new = jnp.maximum(old, jnp.max(scores, axis=1, keepdims=True))
                probs = jnp.exp(scores - twice(new)).astype(BF16)
                ones = jnp.where(low_key, jnp.ones_like(tile), tile)
                accum_s[h] = accum_s[h] * jnp.exp(old - new) + dot(probs, ones)
                peak_s[h] = new

        outs = []
        for h in range(KVH):
            accum = accum_s[h]
            other = swap(accum)
            total = jnp.where(low_lane, accum, other)
            lse_s[slot, h] = peak_s[h] + jnp.log(total)
            mixed = accum / total
            mixed_s[slot, h] = mixed
            outs += [mixed[BLK * j : BLK * j + BLK] for j in range(group)]
        one_low = lane_index(BLK) < HD
        for t in range(HEADS // 2):
            pair = jnp.where(one_low, swap(outs[2 * t]), outs[2 * t + 1])
            low_s[rows, 128 * t : 128 * t + 128] = pair.astype(BF16)
        low_s[rows, QW - HD : QW] = swap(outs[HEADS - 1])[:, :HD].astype(BF16)


def feed_forward(
    meta, x_ref, cot_ref, wa_ref, wgu_ref, wd_ref, act_ref, gres_ref, gb_ref, gain_ref,
    low_s, mixed_s, do_s, delta_s, second_s, grad_gu_s, hidden_s, gm_s,
):
    group = HEADS // KVH
    gain = gain_row(wa_ref, O_AT + HALF)
    high_lane = lane_index(BLK) >= HD
    gain_ref[...] = jnp.zeros_like(gain_ref)

    @pl.loop(0, x_ref.shape[0] // STEP)
    def _(i):
        rows = pl.ds(pl.multiple_of(i * STEP, STEP), STEP)
        w_out = wa_ref[:, O_AT : O_AT + QW]
        residual = x_ref[rows, :].astype(F32) + dot(low_s[rows, :], w_out)
        inv = lax.rsqrt(jnp.mean(residual * residual, axis=1, keepdims=True) + EPS)
        norm = residual * inv
        second = (norm * gain).astype(BF16)
        second_s[:, rows] = second.T
        row = lax.broadcasted_iota(jnp.int32, (BLK, 1), 0)
        living = jnp.concatenate(
            [
                (row < meta[i * (STEP // BLK) + b, 1]).astype(F32)
                for b in range(STEP // BLK)
            ],
            axis=0,
        )
        grad_final = cot_ref[rows, :].astype(F32) * living
        grad_mlp = grad_final.astype(BF16)
        gm_s[rows, :] = grad_mlp
        out = residual
        grad_second = jnp.zeros_like(residual)
        width = 512
        for c in range(0, FF, width):
            w_gate, w_up = wgu_ref[:, c : c + width], wgu_ref[:, FF + c : FF + c + width]
            w_down = wd_ref[c : c + width, :]
            gate, up = dot(second, w_gate), dot(second, w_up)
            sigma = jax.nn.sigmoid(gate)
            swish = gate * sigma
            hidden = (swish * up).astype(BF16)
            hidden_s[rows, c : c + width] = hidden
            out = out + dot(hidden, w_down)
            grad_hidden = dot_nt(grad_mlp, w_down)
            grad_gate = (grad_hidden * up * (sigma * (1.0 + gate * (1.0 - sigma)))).astype(BF16)
            grad_up = (grad_hidden * swish).astype(BF16)
            grad_gu_s[rows, c : c + width] = grad_gate
            grad_gu_s[rows, FF + c : FF + c + width] = grad_up
            grad_second = grad_second + dot_nt(grad_gate, w_gate) + dot_nt(grad_up, w_up)
        act_ref[rows, :] = out.astype(BF16)
        scaled = grad_second * gain
        grad_res = grad_final + inv * (scaled - norm * jnp.mean(scaled * norm, axis=1, keepdims=True))
        gres_ref[rows, :] = grad_res
        grad_branch = grad_res.astype(BF16)
        gb_ref[rows, :QW] = grad_branch
        gb_ref[rows, QW:] = jnp.zeros((STEP, 128 - HD), BF16)
        gain_ref[0:1, :] += jnp.sum(grad_second * norm, axis=0, keepdims=True)
        grad_att = dot_nt(grad_branch, w_out)
        for b in range(STEP // BLK):
            slot = i * (STEP // BLK) + b
            here = pl.ds(pl.multiple_of(i * STEP + b * BLK, BLK), BLK)
            part = slice(b * BLK, (b + 1) * BLK)
            for head in range(HEADS):
                at = 128 * (head // 2)
                if head == HEADS - 1:
                    tile = jnp.concatenate([grad_att[part, at : at + HD]] * 2, axis=1)
                else:
                    tile = grad_att[part, at : at + 128]
                    tile = tile if head % 2 else swap(tile)
                tile = jnp.where(high_lane, tile, 0.0).astype(BF16)
                do_s[here, 128 * head : 128 * head + 128] = tile
                h, j = head // group, head % group
                product = tile.astype(F32) * mixed_s[slot, h, BLK * j : BLK * j + BLK, :]
                delta = jnp.sum(product, axis=1, keepdims=True)
                delta_s[slot, h, BLK * j : BLK * j + BLK, :] = jnp.broadcast_to(delta, (BLK, 128))


def weight_grads(dgu_ref, dd_ref, second_s, grad_gu_s, hidden_s, gm_s):
    width = 512
    for c in range(0, 2 * FF, width):
        dgu_ref[:, c : c + width] = dot(second_s[...], grad_gu_s[:, c : c + width]).astype(BF16)
    for c in range(0, FF, width):
        dd_ref[c : c + width, :] = dot_tn(hidden_s[:, c : c + width], gm_s[...]).astype(BF16)


def attention_backward(meta, q_ref, kv_ref, inner_ref, outer_ref, do_s, lse_s, delta_s, gq_ref, dkv_s, dq_s):
    group = HEADS // KVH
    tall = group * BLK
    dkv_s[...] = jnp.zeros_like(dkv_s)

    @pl.loop(0, q_ref.shape[0] // BLK)
    def _(slot):
        rows = pl.ds(pl.multiple_of(slot * BLK, BLK), BLK)
        dq_s[...] = jnp.zeros_like(dq_s)

        @pl.loop(0, meta[slot, 2])
        def _(chunk):
            bias = chunk_bias(meta, slot, chunk)
            one = pl.ds(pl.multiple_of(meta[slot, 4 + 2 * chunk] * BLK, BLK), BLK)
            two = pl.ds(pl.multiple_of(meta[slot, 5 + 2 * chunk] * BLK, BLK), BLK)
            for h in range(KVH):
                lanes = slice(128 * h, 128 * h + 128)
                tile = key_tile(kv_ref, meta, slot, chunk, h)
                both = jnp.concatenate([stacked(q_ref, rows, h), stacked(do_s, rows, h)], axis=0)
                products = dot_nt(both, tile)
                probs = jnp.exp(products[:tall] + bias - twice(lse_s[slot, h]))
                grads = (probs * (products[tall:] - twice(delta_s[slot, h]))).astype(BF16)
                dq_s[h] += dot(grads, tile)
                sides = jnp.concatenate([grads, probs.astype(BF16)], axis=0)
                terms = dot_tn(sides, both)
                dkv_s[one, lanes] += terms[:BLK]
                dkv_s[two, lanes] += terms[BLK:]

        tables = rope_tables(meta, slot, inner_ref, outer_ref)
        low_lane = lane_index(BLK) < HD
        heads = [
            rope_back(dq_s[h, BLK * j : BLK * j + BLK, :] * SCALE, tables)
            for h in range(KVH)
            for j in range(group)
        ]
        for t in range(HEADS // 2):
            pair = jnp.where(low_lane, heads[2 * t], swap(heads[2 * t + 1]))
            gq_ref[rows, 128 * t : 128 * t + 128] = pair.astype(BF16)
        gq_ref[rows, QW - HD :] = jnp.where(low_lane, heads[HEADS - 1], 0.0).astype(BF16)


def layer_kernel(
    meta, x_ref, cot_ref, q_ref, kv_ref, wa_ref, wgu_ref, wd_ref, inner_ref, outer_ref,
    act_ref, gres_ref, gb_ref, low_ref, gq_ref, dkv_ref, dgu_ref, dd_ref, gain_ref,
    mixed_s, lse_s, delta_s, peak_s, accum_s, do_s, second_s, grad_gu_s, hidden_s, gm_s, dkv_s,
):
    attention_forward(meta, q_ref, kv_ref, mixed_s, low_ref, lse_s, peak_s, accum_s)
    feed_forward(
        meta, x_ref, cot_ref, wa_ref, wgu_ref, wd_ref, act_ref, gres_ref, gb_ref, gain_ref,
        low_ref, mixed_s, do_s, delta_s, second_s, grad_gu_s, hidden_s, gm_s,
    )
    weight_grads(dgu_ref, dd_ref, second_s, grad_gu_s, hidden_s, gm_s)
    attention_backward(
        meta, q_ref, kv_ref, inner_ref, outer_ref, do_s, lse_s, delta_s, gq_ref, dkv_s, accum_s
    )
    dkv_ref[...] = dkv_s[...].astype(BF16)


def layer(meta, tokens, cotangent, queries, keyval, packed, gateup, down, inner, outer):
    rows, slots, group = tokens.shape[0], tokens.shape[0] // BLK, HEADS // KVH
    keys = keyval.shape[0]
    return pl.pallas_call(
        layer_kernel,
        out_shape=(
            jax.ShapeDtypeStruct((rows, D), BF16),
            jax.ShapeDtypeStruct((rows, D), F32),
            jax.ShapeDtypeStruct((rows, QW + HD), BF16),
            jax.ShapeDtypeStruct((rows, QW), BF16),
            jax.ShapeDtypeStruct((rows, QW + HD), BF16),
            jax.ShapeDtypeStruct((keys, 2 * KVW), BF16),
            jax.ShapeDtypeStruct((D, 2 * FF), BF16),
            jax.ShapeDtypeStruct((FF, D), BF16),
            jax.ShapeDtypeStruct((8, D), F32),
        ),
        in_specs=[pl.BlockSpec(memory_space=pltpu.SMEM)] + vmem(9),
        out_specs=tuple(vmem(9)),
        scratch_shapes=[
            pltpu.VMEM((slots, KVH, group * BLK, 128), F32),
            pltpu.VMEM((slots, KVH, group * BLK, 128), F32),
            pltpu.VMEM((slots, KVH, group * BLK, 128), F32),
            pltpu.VMEM((KVH, group * BLK, 128), F32),
            pltpu.VMEM((KVH, group * BLK, 128), F32),
            pltpu.VMEM((rows, 128 * HEADS), BF16),
            pltpu.VMEM((D, rows), BF16),
            pltpu.VMEM((rows, 2 * FF), BF16),
            pltpu.VMEM((rows, FF), BF16),
            pltpu.VMEM((rows, D), BF16),
            pltpu.VMEM((keys, 2 * KVW), F32),
        ],
        compiler_params=pltpu.CompilerParams(vmem_limit_bytes=62 << 20),
        name="layer",
    )(meta, tokens, cotangent, queries, keyval, packed, gateup, down, inner, outer)


def finish_kernel(
    meta, x_ref, wa_ref, gq_ref, dkv_ref, gres_ref, gb_ref, low_ref, gain_ref, inner_ref, outer_ref,
    in_ref, da_ref, normed_s, first_s, values_s, lowt_s,
):
    gain = gain_row(wa_ref, HALF)
    low_lane = lane_index(BLK) < HD
    rows_all = x_ref.shape[0]
    gains = jnp.zeros((1, D), F32)
    for i in range(rows_all // STEP):
        rows = pl.ds(i * STEP, STEP)
        x = x_ref[rows, :].astype(F32)
        inv = lax.rsqrt(jnp.mean(x * x, axis=1, keepdims=True) + EPS)
        norm = x * inv
        normed_s[:, rows] = (norm * gain).astype(BF16).T
        lowt_s[:, rows] = low_ref[rows, :].T
        first_s[rows, :512] = gq_ref[rows, :512]
        for b in range(STEP // BLK):
            here = pl.ds(i * STEP + b * BLK, BLK)
            tables = rope_tables(meta, i * (STEP // BLK) + b, inner_ref, outer_ref)
            tiles = [
                rope_back(dkv_ref[here, 128 * h : 128 * h + 128].astype(F32), tables)
                for h in range(KVH)
            ]
            last = gq_ref[here, 512:640].astype(F32)
            first_s[here, 512:640] = jnp.where(low_lane, last, swap(tiles[0])).astype(BF16)
            first_s[here, 640:768] = jnp.where(low_lane, tiles[1], swap(tiles[2])).astype(BF16)
            values_s[here, :128] = jnp.where(low_lane, 0.0, tiles[0]).astype(BF16)
            values_s[here, 128:] = jnp.where(low_lane, swap(tiles[1]), tiles[2]).astype(BF16)
        grad_normed = dot_nt(first_s[rows, :], wa_ref[:, :HALF]) + dot_nt(
            values_s[rows, :], wa_ref[:, O_AT + 512 : O_AT + HALF]
        )
        scaled = grad_normed * gain
        in_ref[rows, :] = gres_ref[rows, :] + inv * (
            scaled - norm * jnp.mean(scaled * norm, axis=1, keepdims=True)
        )
        gains = gains + jnp.sum(grad_normed * norm, axis=0, keepdims=True)
    for c in range(0, HALF, 256):
        da_ref[:, c : c + 256] = dot(normed_s[...], first_s[:, c : c + 256]).astype(BF16)
    for c in range(0, 512, 256):
        da_ref[:, O_AT + c : O_AT + c + 256] = dot(lowt_s[...], gb_ref[:, c : c + 256]).astype(BF16)
    da_ref[:, O_AT + 512 : O_AT + 640] = (
        dot(lowt_s[...], gb_ref[:, 512:640]) + dot(normed_s[...], values_s[:, :128])
    ).astype(BF16)
    da_ref[:, O_AT + 640 : O_AT + HALF] = dot(normed_s[...], values_s[:, 128:]).astype(BF16)
    da_ref[:, HALF:O_AT] = jnp.broadcast_to(gains, (128, D)).T.astype(BF16)
    da_ref[:, O_AT + HALF :] = jnp.broadcast_to(gain_ref[0:1, :], (128, D)).T.astype(BF16)


def finish(meta, tokens, packed, gq, dkv, gres, gb, low, gain, inner, outer):
    rows = tokens.shape[0]
    return pl.pallas_call(
        finish_kernel,
        out_shape=(
            jax.ShapeDtypeStruct((rows, D), F32),
            jax.ShapeDtypeStruct((D, WIDE_A), BF16),
        ),
        in_specs=[pl.BlockSpec(memory_space=pltpu.SMEM)] + vmem(10),
        out_specs=tuple(vmem(2)),
        scratch_shapes=[
            pltpu.VMEM((D, rows), BF16),
            pltpu.VMEM((rows, HALF), BF16),
            pltpu.VMEM((rows, 256), BF16),
            pltpu.VMEM((QW, rows), BF16),
        ],
        compiler_params=pltpu.CompilerParams(vmem_limit_bytes=48 << 20),
        name="finish",
    )(meta, tokens, packed, gq, dkv, gres, gb, low, gain, inner, outer)


def pack(w_query, w_keyval, w_out, w_gateup, w_down, norm_gains):
    rows = w_query.shape[0]
    spread = [jnp.broadcast_to(norm_gains[:, g : g + 1], (rows, 128)) for g in range(2)]
    packed = jnp.concatenate(
        [w_query, w_keyval[:, 0], spread[0], w_out, w_keyval[:, 1], spread[1]], axis=1
    )
    return packed.astype(BF16), w_gateup.reshape(rows, 2 * FF).astype(BF16), w_down.astype(BF16)


def for_sending(value):
    return jax.tree.map(lambda a: a.astype(jnp.bfloat16) if a.dtype == jnp.float32 else a, value)


def orthogonal(matrix):
    flipped = matrix.shape[0] > matrix.shape[1]
    iterate = matrix.T if flipped else matrix
    iterate = iterate / (jnp.sqrt(jnp.sum(iterate * iterate)) + 1e-07)
    for turn in range(NS_STEPS):
        gram_matrix = jnp.dot(iterate, iterate.T, precision=lax.Precision.HIGHEST)
        polynomial = COEF_B * gram_matrix + COEF_C * jnp.dot(
            gram_matrix, gram_matrix, precision=lax.Precision.HIGHEST
        )
        iterate = COEF_A * iterate + jnp.dot(polynomial, iterate, precision=lax.Precision.HIGHEST)
    return iterate.T if flipped else iterate


def muon_step(matrix):
    return MUON_RATE * math.sqrt(max(matrix.shape[0], matrix.shape[1])) * orthogonal(matrix)


def owner_branch(matrix_rows, matrix_cols, widest, received):
    group_size = received.shape[0]
    shard_size = matrix_rows * matrix_cols // group_size
    full_matrix = received[:, :shard_size].reshape(matrix_rows, matrix_cols)
    update_rows = muon_step(full_matrix).reshape(group_size, shard_size)
    return jnp.pad(update_rows, ((0, 0), (0, widest - shard_size)))


def zero_branch(received):
    return jnp.zeros_like(received)


def muon_exchange(pieces):
    fsdp_size, fsdp_index = lax.axis_size("fsdp"), lax.axis_index("fsdp")
    flat_sizes = [piece.size for piece in pieces]
    widest = max(flat_sizes)
    padded = [jnp.pad(piece.reshape(-1), (0, widest - piece.size)) for piece in pieces]
    outgoing = jnp.stack(padded + [jnp.zeros((widest,), F32)] * (fsdp_size - len(pieces)))
    received = lax.all_to_all(
        outgoing.astype(BF16), "fsdp", split_axis=0, concat_axis=0, tiled=True
    ).astype(F32)
    branches = [
        partial(owner_branch, piece.shape[0] * fsdp_size, piece.shape[1], widest)
        for piece in pieces
    ] + [zero_branch]
    update_rows = lax.switch(jnp.minimum(fsdp_index, len(pieces)), branches, received)
    returned = lax.all_to_all(
        update_rows.astype(BF16), "fsdp", split_axis=0, concat_axis=0, tiled=True
    ).astype(F32)
    return [returned[m, : flat_sizes[m]].reshape(pieces[m].shape) for m in range(len(pieces))]


def gather_rows_xla(shard):
    return lax.all_gather(shard, "fsdp", axis=0, tiled=True)


def reduce_rows_xla(grads):
    return lax.psum(lax.psum_scatter(grads, "fsdp", scatter_dimension=0, tiled=True), "dp")


class Place:
    def __init__(self, lines):
        self.f, self.d = lax.axis_index("fsdp"), lax.axis_index("dp")
        self.line, self.column = self.f // 2, self.f % 2
        self.x, self.core = self.d // 2, self.d % 2
        self.lines = lines
        self.sibling = (self.f, self.d + 1 - 2 * self.core)
        self.across = (self.f, self.core + 2 * (1 - self.x))
        self.beside = (self.f + 1 - 2 * self.column, self.d)
        self.above = (self.f + 2, self.d)
        self.below = (self.f - 2, self.d)


def remote(source, target, send_sem, recv_sem, device):
    return pltpu.make_async_remote_copy(
        src_ref=source, dst_ref=target, send_sem=send_sem, recv_sem=recv_sem,
        device_id=device, device_id_type=pl.DeviceIdType.MESH,
    )


def greet(place, chips=True):
    barrier = pltpu.get_barrier_semaphore()

    def signal(device):
        pl.semaphore_signal(barrier, inc=1, device_id=device, device_id_type=pl.DeviceIdType.MESH)

    signal(place.sibling)
    signal(place.across)
    if not chips:
        pl.semaphore_wait(barrier, 2)
        return
    signal(place.beside)
    pl.when(place.line > 0)(lambda: signal(place.below))
    pl.when(place.line < place.lines - 1)(lambda: signal(place.above))
    ends = (place.line == 0).astype(jnp.int32) + (place.line == place.lines - 1).astype(jnp.int32)
    pl.semaphore_wait(barrier, 5 - ends)


PARTS = 4


def half_parts(packed, gateup, down, core):
    wide, tall = packed.shape[1] // 2, down.shape[0] // 2
    at = core * FF
    return (
        packed.at[:, pl.ds(pl.multiple_of(core * wide, 128), wide)],
        gateup.at[:, pl.ds(pl.multiple_of(at, 128), FF // 2)],
        gateup.at[:, pl.ds(pl.multiple_of(at + FF // 2, 128), FF // 2)],
        down.at[pl.ds(pl.multiple_of(core * tall, 16), tall), :],
    )


def gather_kernel(
    lines, wq_ref, wkv_ref, wo_ref, wgu_ref, wd_ref, gains_ref, a_out, gu_out, d_out, a_ref, gu_ref, d_ref,
    own_sem, in_sem, pair_sem, up_sem, down_sem, side_sem, cross_sem, mate_sem,
):
    place = Place(lines)
    rows = a_ref.shape[0]
    for side, w_ref in enumerate((wq_ref, wo_ref)):
        at = side * O_AT
        a_ref[:, at : at + QW] = w_ref[...].astype(BF16)
        a_ref[:, at + QW : at + HALF] = wkv_ref[:, side, :].astype(BF16)
        spread = jnp.broadcast_to(gains_ref[:, side : side + 1], (rows, 128))
        a_ref[:, at + HALF : at + O_AT] = spread.astype(BF16)
        gu_ref[:, side * FF : side * FF + FF] = wgu_ref[:, side, :].astype(BF16)
    d_ref[...] = wd_ref[...].astype(BF16)
    own = [
        pltpu.make_async_copy(src, dst.at[place.f], own_sem.at[i])
        for i, (src, dst) in enumerate(((a_ref, a_out), (gu_ref, gu_out), (d_ref, d_out)))
    ]
    for copy in own:
        copy.start()
    greet(place)

    def full(shard, core):
        return half_parts(a_out.at[shard], gu_out.at[shard], d_out.at[shard], core)

    mine = half_parts(a_ref, gu_ref, d_ref, place.core)

    def send(shard, k, sems, device, recv, source=None):
        target = full(shard, place.core)[k]
        return remote(target if source is None else source, target, sems.at[shard, k], recv.at[shard, k], device)

    def arrived(shard, k):
        send(shard, k, up_sem, place.sibling, in_sem).wait_recv()

    def to_pair(shard, k):
        return send(shard, k, mate_sem, place.sibling, pair_sem)

    def on_z(t, k, action):
        if t == 0:
            pl.when(place.line < lines - 1)(
                lambda: action(send(place.f, k, up_sem, place.above, in_sem, mine[k]))
            )
            pl.when(place.line > 0)(
                lambda: action(send(place.f, k, down_sem, place.below, in_sem, mine[k]))
            )
            pl.when(place.x == k % 2)(
                lambda: action(send(place.f, k, side_sem, place.beside, in_sem, mine[k]))
            )
            return
        for sign in (-1, 1):
            shard = place.f + 2 * sign * t
            there = place.line + sign * t

            def go(shard=shard, sign=sign):
                action(None, shard)
                if sign < 0:
                    pl.when(place.line < lines - 1)(
                        lambda: action(send(shard, k, up_sem, place.above, in_sem))
                    )
                else:
                    pl.when(place.line > 0)(
                        lambda: action(send(shard, k, down_sem, place.below, in_sem))
                    )
                pl.when(place.x == k % 2)(
                    lambda: action(send(shard, k, side_sem, place.beside, in_sem))
                )
                action(to_pair(shard, k))

            pl.when((there >= 0) & (there < lines))(go)

    def others(t, run):
        base = place.beside[0]
        if t == 0:
            run(base)
            return
        for sign in (-1, 1):
            there = place.line + sign * t
            pl.when((there >= 0) & (there < lines))(lambda sign=sign: run(base + 2 * sign * t))

    def on_side(t, k, action):
        def run(shard):
            action(None, shard)
            action(send(shard, k, cross_sem, place.across, in_sem))
            action(to_pair(shard, k))

        pl.when(place.x == k % 2)(lambda: others(t, run))

    def on_cross(t, k, action):
        def run(shard):
            action(None, shard)
            action(to_pair(shard, k))

        pl.when(place.x != k % 2)(lambda: others(t, run))

    def start(k):
        def action(copy, shard=None):
            if copy is None:
                arrived(shard, k)
            else:
                copy.start()

        return action

    def finish_send(copy, shard=None):
        if copy is not None:
            copy.wait_send()

    for t in range(lines + 2):
        for k in range(PARTS):
            if t < lines:
                on_z(t, k, start(k))
            if 0 <= t - 1 < lines:
                on_side(t - 1, k, start(k))
            if 0 <= t - 2 < lines:
                on_cross(t - 2, k, start(k))
    for t in range(lines):
        for k in range(PARTS):
            on_z(t, k, finish_send)
            on_side(t, k, finish_send)
            on_cross(t, k, finish_send)
            pair_half = 1 - place.core

            def got(shard, k=k):
                target = full(shard, pair_half)[k]
                remote(target, target, mate_sem.at[shard, k], pair_sem.at[shard, k], place.sibling).wait_recv()

            others(t, got)
            if t > 0:
                for sign in (-1, 1):
                    there = place.line + sign * t
                    pl.when((there >= 0) & (there < lines))(
                        lambda sign=sign: got(place.f + 2 * sign * t)
                    )
    for copy in own:
        copy.wait()


def gather_weights_remote(weights, gains, count):
    rows, tall = weights[0].shape[0], weights[4].shape[0]
    sems = pltpu.SemaphoreType.DMA((count, PARTS))
    shapes = ((rows, WIDE_A), (rows, 2 * FF), (tall, D))
    return pl.pallas_call(
        partial(gather_kernel, count // 2),
        out_shape=tuple(jax.ShapeDtypeStruct((count,) + s, BF16) for s in shapes),
        in_specs=vmem(6),
        out_specs=(pl.BlockSpec(memory_space=pl.ANY),) * 3,
        scratch_shapes=[pltpu.VMEM(s, BF16) for s in shapes]
        + [pltpu.SemaphoreType.DMA((3,))]
        + [sems] * 7,
        compiler_params=pltpu.CompilerParams(
            collective_id=0, has_side_effects=True, vmem_limit_bytes=32 << 20
        ),
        name="gather_weights",
    )(*weights, gains)


CUTS = 3


def gather_keyval_kernel(kv_ref, out_ref, own_sem, in_sem, pair_sem, cross_send, mate_send):
    place = Place(4)
    piece = kv_ref.shape[0] // CUTS
    own = pltpu.make_async_copy(kv_ref, out_ref.at[place.d], own_sem)
    own.start()
    greet(place, False)
    far = place.across[1]
    near = place.sibling[1]

    def rows(k):
        return pl.ds(k * piece, piece)

    crossing = [
        remote(kv_ref.at[rows(k)], out_ref.at[place.d, rows(k)], cross_send.at[k], in_sem.at[k], place.across)
        for k in range(CUTS)
    ]
    pairing = remote(kv_ref, out_ref.at[place.d], mate_send.at[CUTS], pair_sem.at[CUTS], place.sibling)
    for copy in crossing:
        copy.start()
    pairing.start()
    passing = []
    for k in range(CUTS):
        crossing[k].wait_recv()
        here = out_ref.at[far, rows(k)]
        copy = remote(here, here, mate_send.at[k], pair_sem.at[k], place.sibling)
        copy.start()
        passing.append(copy)
    pairing.wait()
    for k in range(CUTS):
        crossing[k].wait_send()
        passing[k].wait()
    own.wait()


def gather_keyval_remote(keyval):
    return pl.pallas_call(
        gather_keyval_kernel,
        out_shape=jax.ShapeDtypeStruct((4,) + keyval.shape, keyval.dtype),
        in_specs=[pl.BlockSpec(memory_space=pl.ANY)],
        out_specs=pl.BlockSpec(memory_space=pl.ANY),
        scratch_shapes=[
            pltpu.SemaphoreType.DMA,
            pltpu.SemaphoreType.DMA((CUTS,)),
            pltpu.SemaphoreType.DMA((CUTS + 1,)),
            pltpu.SemaphoreType.DMA((CUTS,)),
            pltpu.SemaphoreType.DMA((CUTS + 1,)),
        ],
        compiler_params=pltpu.CompilerParams(collective_id=1, has_side_effects=True),
        name="gather_keyval",
    )(keyval).reshape(4 * keyval.shape[0], keyval.shape[1])


def added(one, two):
    return one.astype(F32) + two.astype(F32)


def reduce_keyval_kernel(part_ref, out_ref, pair_s, far_s, cross_s, pair_recv, cross_recv, pair_send, cross_send):
    place = Place(4)
    greet(place, False)
    piece = out_ref.shape[0] // CUTS
    far = place.across[1]
    near_core = 1 - place.core
    targets = (near_core + 2 * (1 - place.x), near_core + 2 * place.x)

    def rows(k):
        return pl.ds(k * piece, piece)

    pairing = [
        [
            remote(part_ref.at[targets[w], rows(k)], pair_s.at[w, rows(k)], pair_send.at[w, k], pair_recv.at[w, k], place.sibling)
            for k in range(CUTS)
        ]
        for w in range(2)
    ]
    for w in range(2):
        for copy in pairing[w]:
            copy.start()
    crossing = []
    for k in range(CUTS):
        pairing[0][k].wait_recv()
        far_s[rows(k)] = added(part_ref[far, rows(k)], pair_s[0, rows(k)]).astype(BF16)
        copy = remote(far_s.at[rows(k)], cross_s.at[rows(k)], cross_send.at[k], cross_recv.at[k], place.across)
        copy.start()
        crossing.append(copy)
    for k in range(CUTS):
        pairing[1][k].wait_recv()
        crossing[k].wait_recv()
        mine = added(part_ref[place.d, rows(k)], pair_s[1, rows(k)])
        out_ref[rows(k)] = (mine + cross_s[rows(k)].astype(F32)).astype(BF16)
    for k in range(CUTS):
        pairing[0][k].wait_send()
        pairing[1][k].wait_send()
        crossing[k].wait_send()


def reduce_keyval_remote(dkv):
    rows, width = dkv.shape[0] // 4, dkv.shape[1]
    return pl.pallas_call(
        reduce_keyval_kernel,
        out_shape=jax.ShapeDtypeStruct((rows, width), BF16),
        in_specs=vmem(1),
        out_specs=vmem(1)[0],
        scratch_shapes=[
            pltpu.VMEM((2, rows, width), BF16),
            pltpu.VMEM((rows, width), BF16),
            pltpu.VMEM((rows, width), BF16),
            pltpu.SemaphoreType.DMA((2, CUTS)),
            pltpu.SemaphoreType.DMA((CUTS,)),
            pltpu.SemaphoreType.DMA((2, CUTS)),
            pltpu.SemaphoreType.DMA((CUTS,)),
        ],
        compiler_params=pltpu.CompilerParams(
            collective_id=2, has_side_effects=True, vmem_limit_bytes=32 << 20
        ),
        name="reduce_keyval",
    )(dkv.reshape(4, rows, width))


def visit_order(lines):
    return [sorted(range(lines), key=lambda other: (-abs(other - line), -other)) for line in range(lines)]


def sum_kernel(
    lines, a_ref, gu_ref, d_ref, a_out, gu_out, d_out,
    a_s, gu_s, d_s, a_in, gu_in, d_in, pair_recv, recv, last_recv, pair_send, send, last_send,
):
    place = Place(lines)
    greet(place)
    order_table = visit_order(lines)
    home = lines * 2

    def order(t):
        spot = jnp.int32(0)
        for line in range(lines):
            spot = spot + order_table[line][t] * (place.line == line).astype(jnp.int32)
        return spot

    def pieces(shard, core):
        return half_parts(a_ref.at[shard], gu_ref.at[shard], d_ref.at[shard], core)

    def running(shard):
        half = FF // 2
        return (
            a_s.at[shard], gu_s.at[shard, :, pl.ds(0, half)], gu_s.at[shard, :, pl.ds(half, half)],
            d_s.at[shard],
        )

    def inbox(way, spot):
        half = FF // 2
        return (
            a_in.at[way, spot], gu_in.at[way, spot, :, pl.ds(0, half)],
            gu_in.at[way, spot, :, pl.ds(half, half)], d_in.at[way, spot],
        )

    def to_pair(shard, k):
        return remote(
            pieces(shard, 1 - place.core)[k], running(shard)[k],
            pair_send.at[shard, k], pair_recv.at[shard, k], place.sibling,
        )

    def pass_on(shard, k, way, spot, device):
        return remote(
            running(shard)[k], inbox(way, spot)[k], send.at[way, spot, k], recv.at[way, spot, k], device
        )

    def add(shard, k, other):
        total = running(shard)[k]
        total[...] = added(total[...], other[...]).astype(BF16)

    def collect(shard, k, way, spot):
        pass_on(shard, k, way, spot, place.sibling).wait_recv()
        add(shard, k, inbox(way, spot)[k])

    def first_sum(shard, k):
        to_pair(shard, k).wait_recv()
        add(shard, k, pieces(shard, place.core)[k])

    def stage_pair(t):
        spot = order(t)
        shard = 2 * spot + 1 - place.column
        for k in range(PARTS):
            first_sum(shard, k)
            pl.when(place.x != k % 2)(lambda k=k: pass_on(shard, k, 0, spot, place.across).start())

    def stage_side(t):
        spot = order(t)
        shard = 2 * spot + 1 - place.column
        for k in range(PARTS):

            def go(k=k):
                collect(shard, k, 0, spot)
                pass_on(shard, k, 1, spot, place.beside).start()

            pl.when(place.x == k % 2)(go)
        for k in range(PARTS):
            first_sum(2 * spot + place.column, k)

    def stage_line(t):
        spot = order(t)
        shard = 2 * spot + place.column
        for k in range(PARTS):
            pl.when(place.x == k % 2)(lambda k=k: collect(shard, k, 1, spot))

            def up(k=k):
                pl.when(place.line > 0)(lambda: collect(shard, k, 2, spot))
                pass_on(shard, k, 2, spot, place.above).start()

            def down(k=k):
                pl.when(place.line < lines - 1)(lambda: collect(shard, k, 3, spot))
                pass_on(shard, k, 3, spot, place.below).start()

            if t < lines - 1:
                pl.when(spot > place.line)(up)
                pl.when(spot < place.line)(down)
            else:
                pl.when(place.line > 0)(lambda k=k: collect(shard, k, 2, spot))
                pl.when(place.line < lines - 1)(lambda k=k: collect(shard, k, 3, spot))
                last(k).start()

    def last(k):
        return remote(
            running(place.f)[k], inbox(4, 0)[k], last_send.at[0, k], last_recv.at[0, k], place.across
        )

    def share(k):
        target = half_parts(a_out, gu_out, d_out, place.core)[k]
        return remote(target, target, last_send.at[1, k], last_recv.at[1, k], place.sibling)

    for t in range(lines):
        spot = order(t)
        for column in (1 - place.column, place.column):
            for k in range(PARTS):
                to_pair(2 * spot + column, k).start()
    for t in range(lines + 2):
        if t < lines:
            stage_pair(t)
        if 0 <= t - 1 < lines:
            stage_side(t - 1)
        if 0 <= t - 2 < lines:
            stage_line(t - 2)
    for k in range(PARTS):
        last(k).wait_recv()
        target = half_parts(a_out, gu_out, d_out, place.core)[k]
        target[...] = added(running(place.f)[k][...], inbox(4, 0)[k][...]).astype(BF16)
        share(k).start()
    for k in range(PARTS):
        target = half_parts(a_out, gu_out, d_out, 1 - place.core)[k]
        remote(target, target, last_send.at[1, k], last_recv.at[1, k], place.sibling).wait_recv()
        share(k).wait_send()
        last(k).wait_send()
    for t in range(lines):
        spot = order(t)
        for k in range(PARTS):
            for column in range(2):
                to_pair(2 * spot + column, k).wait_send()
            shard = 2 * spot + 1 - place.column
            pl.when(place.x != k % 2)(lambda k=k: pass_on(shard, k, 0, spot, place.across).wait_send())
            pl.when(place.x == k % 2)(lambda k=k: pass_on(shard, k, 1, spot, place.beside).wait_send())
            if t < lines - 1:
                shard = 2 * spot + place.column
                pl.when(spot > place.line)(lambda k=k: pass_on(shard, k, 2, spot, place.above).wait_send())
                pl.when(spot < place.line)(lambda k=k: pass_on(shard, k, 3, spot, place.below).wait_send())


def reduce_grads_remote(grads, count):
    lines = count // 2
    grads = tuple(g.reshape(count, g.shape[0] // count, g.shape[1]) for g in grads)
    a_shape, gu_shape, d_shape = (g.shape[1:] for g in grads)
    halves = ((a_shape[0], a_shape[1] // 2), (gu_shape[0], FF), (d_shape[0] // 2, d_shape[1]))
    return pl.pallas_call(
        partial(sum_kernel, lines),
        out_shape=tuple(jax.ShapeDtypeStruct(g.shape[1:], BF16) for g in grads),
        in_specs=vmem(3),
        out_specs=tuple(vmem(3)),
        scratch_shapes=[pltpu.VMEM((count,) + h, BF16) for h in halves]
        + [pltpu.VMEM((5, lines) + h, BF16) for h in halves]
        + [
            pltpu.SemaphoreType.DMA((count, PARTS)),
            pltpu.SemaphoreType.DMA((4, lines, PARTS)),
            pltpu.SemaphoreType.DMA((2, PARTS)),
            pltpu.SemaphoreType.DMA((count, PARTS)),
            pltpu.SemaphoreType.DMA((4, lines, PARTS)),
            pltpu.SemaphoreType.DMA((2, PARTS)),
        ],
        compiler_params=pltpu.CompilerParams(
            collective_id=3, has_side_effects=True, vmem_limit_bytes=60 << 20
        ),
        name="sum_grads",
    )(*grads)


def own_kernels():
    return lax.axis_size("fsdp") == 8 and lax.axis_size("dp") == 4


def gather_weights(weights, gains):
    if not own_kernels():
        return tuple(gather_rows_xla(s) for s in pack(*weights, gains))
    full = gather_weights_remote(weights, gains, lax.axis_size("fsdp"))
    return tuple(f.reshape(f.shape[0] * f.shape[1], f.shape[2]) for f in full)


def gather_keyval(keyval):
    if not own_kernels():
        return lax.all_gather(keyval, "dp", axis=0, tiled=True)
    return gather_keyval_remote(keyval)


def reduce_keyval(dkv):
    if not own_kernels():
        return lax.psum_scatter(dkv, "dp", scatter_dimension=0, tiled=True)
    return reduce_keyval_remote(dkv)


def reduce_grads(grads):
    if not own_kernels():
        return tuple(reduce_rows_xla(g) for g in grads)
    return reduce_grads_remote(grads, lax.axis_size("fsdp"))


WIDE_AT, TALL_AT = (2, 5), 3
SQUARE_AT, NARROW_AT = (0, 7), (6, 1)
NARROW = 256


def by_core(pair, core):
    return pair[0] + (pair[1] - pair[0]) * core


def greet_plane(place, count):
    barrier = pltpu.get_barrier_semaphore()
    pl.semaphore_signal(barrier, inc=1, device_id=place.sibling, device_id_type=pl.DeviceIdType.MESH)
    for step in range(1, count):
        f = lax.rem(place.f + step, count)
        for core in range(2):
            pl.semaphore_signal(
                barrier, inc=1, device_id=(f, 2 * place.x + core), device_id_type=pl.DeviceIdType.MESH
            )
    pl.semaphore_wait(barrier, 2 * count - 1)


def newton_schulz(x_s, low_s, gram_s, gram_low_s, poly_s):
    size, width = x_s.shape
    cuts = [(at, min(256, size - at)) for at in range(0, size, 256)]

    @pl.loop(0, NS_STEPS)
    def _(step):
        shift = jnp.where(step >= NS_STEPS - 2, 1.0, 0.0)
        for at, wide in cuts:
            gram = dot_nt(low_s[...], low_s[at : at + wide, :])
            row = lax.broadcasted_iota(jnp.int32, (size, wide), 0)
            column = lax.broadcasted_iota(jnp.int32, (size, wide), 1) + at
            gram = gram - jnp.where(row == column, shift, 0.0)
            gram_s[:, at : at + wide] = gram
            gram_low_s[:, at : at + wide] = gram.astype(BF16)
        for at, wide in cuts:
            square = dot(gram_low_s[...], gram_low_s[:, at : at + wide])
            poly = (COEF_B + 2.0 * COEF_C * shift) * gram_s[:, at : at + wide] + COEF_C * square
            poly_s[:, at : at + wide] = poly.astype(BF16)
        keep = COEF_A + COEF_B * shift + COEF_C * shift * shift
        for at in range(0, width, 256):
            lanes = slice(at, at + 256)
            new = keep * x_s[:, lanes] + dot(poly_s[...], low_s[:, lanes])
            x_s[:, lanes] = new
            low_s[:, lanes] = new.astype(BF16)


def muon_kernel(
    count, a_ref, gu_ref, d_ref, mq_ref, mkv_ref, mo_ref, mgu_ref, md_ref,
    sq_out, nk_out, gu_out, d_out,
    my_gu, my_sq, my_nk, my_d, wide_s, sq_s, nk_s, tall_s, x_s, low_s, gram_s, gram_low_s, poly_s,
    in_send, in_recv, own_sem, out_send, out_recv, pair_send, pair_recv,
):
    place = Place(count // 2)
    greet_plane(place, count)
    rows, tall = my_gu.shape[0], my_d.shape[0]

    def moment(momentum, grad):
        return (MOMENTUM_DECAY * momentum + grad.astype(F32)).astype(BF16)

    my_nk[...] = jnp.zeros_like(my_nk)

    def moments_of(core, m_square):
        my_gu[...] = moment(mgu_ref[:, core, :], gu_ref[:, core * FF : core * FF + FF])
        at = core * O_AT
        my_sq[...] = moment(m_square[...], a_ref[:, at : at + QW])
        my_nk[:, :KVW] = moment(mkv_ref[:, core, :], a_ref[:, at + QW : at + HALF])
        part = slice(core * tall, (core + 1) * tall)
        my_d[...] = moment(md_ref[part, :], d_ref[part, :])

    pl.when(place.core == 0)(lambda: moments_of(0, mq_ref))
    pl.when(place.core == 1)(lambda: moments_of(1, mo_ref))

    tall_rows = pl.ds(pl.multiple_of(place.core * tall, 16), tall)
    wide_at, sq_at, nk_at = (by_core(p, place.core) for p in (WIDE_AT, SQUARE_AT, NARROW_AT))
    tall_core = 2 * place.x
    routes = (
        (my_gu, wide_s.at[place.f], wide_at, place.d),
        (my_d, tall_s.at[place.f, tall_rows], TALL_AT, tall_core),
        (my_sq, sq_s.at[place.f], sq_at, place.d),
        (my_nk, nk_s.at[place.f], nk_at, place.d),
    )

    def each_route(far, near):
        for i, (source, target, f, d) in enumerate(routes):
            here = (place.f == f) & (place.d == d)
            recv = in_recv.at[i, place.f] if i != 1 else in_recv.at[i, place.f + count * place.core]
            pl.when(jnp.logical_not(here))(
                lambda i=i, source=source, target=target, f=f, d=d, recv=recv: far(
                    remote(source, target, in_send.at[i], recv, (f, d))
                )
            )
            pl.when(here)(
                lambda i=i, source=source, target=target: near(
                    pltpu.make_async_copy(source, target, own_sem.at[i])
                )
            )

    each_route(lambda copy: copy.start(), lambda copy: copy.start())
    each_route(lambda copy: copy.wait_send(), lambda copy: copy.wait())

    def received(i, slot_of):
        for step in range(1, count):
            f = lax.rem(place.f + step, count)
            target = slot_of(f)
            remote(target, target, in_send.at[i], in_recv.at[i, f], place.sibling).wait_recv()

    def received_tall():
        for step in range(count):
            f = lax.rem(place.f + step, count)
            for core in range(2):
                if step == 0 and core == 0:
                    continue
                target = tall_s.at[f, pl.ds(core * tall, tall)]
                remote(target, target, in_send.at[1], in_recv.at[1, f + count * core], place.sibling).wait_recv()

    def scaled():
        total = jnp.zeros((1, 1), F32)
        for at in range(0, FF, 256):
            part = x_s[:, at : at + 256]
            total = total + jnp.sum(jnp.sum(part * part, axis=0, keepdims=True), axis=1, keepdims=True)
        factor = 1.0 / (jnp.sqrt(total) + 1e-07)
        for at in range(0, FF, 256):
            part = x_s[:, at : at + 256] * factor
            x_s[:, at : at + 256] = part
            low_s[:, at : at + 256] = part.astype(BF16)

    is_wide, is_square, is_narrow = (place.f == at for at in (wide_at, sq_at, nk_at))
    is_tall = (place.f == TALL_AT) & (place.core == 0)
    is_small = is_square | is_narrow

    @pl.when(is_wide)
    def _():
        received(0, lambda f: wide_s.at[f])
        for f in range(count):
            x_s[f * rows : (f + 1) * rows, :] = wide_s[f].astype(F32)

    @pl.when(is_tall)
    def _():
        received_tall()
        for f in range(0, count, 2):
            pair = jnp.concatenate([tall_s[f], tall_s[f + 1]], axis=0).astype(F32)
            x_s[:, 2 * f * tall : 2 * (f + 2) * tall] = pair.T

    @pl.when(is_small)
    def _():
        x_s[...] = jnp.zeros_like(x_s)

    @pl.when(is_square)
    def _():
        received(2, lambda f: sq_s.at[f])
        for f in range(count):
            x_s[f * rows : (f + 1) * rows, :QW] = sq_s[f].astype(F32)

    @pl.when(is_narrow)
    def _():
        received(3, lambda f: nk_s.at[f])
        for f in range(count):
            x_s[f * rows : (f + 1) * rows, :NARROW] = nk_s[f].astype(F32)

    @pl.when(is_wide | is_tall | is_small)
    def _():
        scaled()
        newton_schulz(x_s, low_s, gram_s, gram_low_s, poly_s)

    rate = MUON_RATE * math.sqrt(FF)
    small_rate = MUON_RATE * math.sqrt(D)

    def back(i, f, core):
        source = (
            wide_s.at[f], tall_s.at[f, pl.ds(core * tall, tall)] if i == 1 else None, sq_s.at[f], nk_s.at[f],
        )[i]
        return source, landing(i, core), (f, 2 * place.x + core)

    def landing(i, core):
        if i == 1:
            start = core * tall if isinstance(core, int) else pl.multiple_of(core * tall, 16)
            return d_out.at[pl.ds(start, tall)]
        return (gu_out, None, sq_out, nk_out)[i].at[core]

    def give(i, cores, act):
        for step in range(count):
            f = lax.rem(place.f + step, count)
            for n, core in enumerate(cores):
                source, target, device = back(i, f, core)
                if step == 0 and n == 0:
                    copy = pltpu.make_async_copy(source, target, own_sem.at[i])
                    act(copy, True)
                else:
                    slot = f + count * n
                    act(remote(source, target, out_send.at[i, slot], out_recv.at[i], device), False)

    def given(i, cores):
        give(i, cores, lambda copy, own: copy.start())
        give(i, cores, lambda copy, own: copy.wait() if own else copy.wait_send())

    @pl.when(is_wide)
    def _():
        for f in range(count):
            wide_s[f] = (x_s[f * rows : (f + 1) * rows, :] * rate).astype(BF16)
        given(0, (place.core,))

    @pl.when(is_tall)
    def _():
        for f in range(0, count, 2):
            pair = (x_s[:, 2 * f * tall : 2 * (f + 2) * tall] * rate).T
            tall_s[f] = pair[: 2 * tall].astype(BF16)
            tall_s[f + 1] = pair[2 * tall :].astype(BF16)
        given(1, (0, 1))

    @pl.when(is_square)
    def _():
        for f in range(count):
            sq_s[f] = (x_s[f * rows : (f + 1) * rows, :QW] * small_rate).astype(BF16)
        given(2, (place.core,))

    @pl.when(is_narrow)
    def _():
        for f in range(count):
            nk_s[f] = (x_s[f * rows : (f + 1) * rows, :NARROW] * small_rate).astype(BF16)
        given(3, (place.core,))

    makers = (is_wide, is_tall, is_square, is_narrow)

    def hand_over(i, core):
        target = landing(i, core)
        return remote(target, target, pair_send.at[i], pair_recv.at[i], place.sibling)

    for i in (2, 3, 1, 0):
        target = landing(i, place.core)

        def take(i=i, target=target):
            remote(target, target, pair_send.at[i], out_recv.at[i], place.sibling).wait_recv()

        pl.when(jnp.logical_not(makers[i]))(take)
        hand_over(i, place.core).start()
    for i in range(4):
        hand_over(i, 1 - place.core).wait_recv()
        hand_over(i, place.core).wait_send()


def muon_remote(grads, momenta, count):
    rows, tall = grads[0].shape[0], grads[2].shape[0] // 2
    pieces = ((rows, FF), (rows, QW), (rows, NARROW), (tall, D))
    return pl.pallas_call(
        partial(muon_kernel, count),
        out_shape=(
            jax.ShapeDtypeStruct((2, rows, QW), BF16),
            jax.ShapeDtypeStruct((2, rows, NARROW), BF16),
            jax.ShapeDtypeStruct((2, rows, FF), BF16),
            jax.ShapeDtypeStruct((2 * tall, D), BF16),
        ),
        in_specs=vmem(8),
        out_specs=tuple(vmem(4)),
        scratch_shapes=[pltpu.VMEM(p, BF16) for p in pieces]
        + [pltpu.VMEM((count,) + p, BF16) for p in pieces[:3]]
        + [
            pltpu.VMEM((count, 2 * tall, D), BF16),
            pltpu.VMEM((D, FF), F32),
            pltpu.VMEM((D, FF), BF16),
            pltpu.VMEM((D, D), F32),
            pltpu.VMEM((D, D), BF16),
            pltpu.VMEM((D, D), BF16),
            pltpu.SemaphoreType.DMA((4,)),
            pltpu.SemaphoreType.DMA((4, 2 * count)),
            pltpu.SemaphoreType.DMA((4,)),
            pltpu.SemaphoreType.DMA((4, 2 * count)),
            pltpu.SemaphoreType.DMA((4,)),
            pltpu.SemaphoreType.DMA((4,)),
            pltpu.SemaphoreType.DMA((4,)),
        ],
        compiler_params=pltpu.CompilerParams(
            collective_id=4, has_side_effects=True, vmem_limit_bytes=56 << 20
        ),
        name="muon",
    )(*grads, *momenta)


def outputs_kernel(
    gain_rate, a_ref, gu_ref, d_ref, sq_ref, nk_ref, ugu_ref, ud_ref,
    gains_ref, gainm_ref, wq_ref, wkv_ref, wo_ref, wgu_ref, wd_ref,
    mq_ref, mkv_ref, mo_ref, mgu_ref, md_ref,
    gg_ref, gm_ref, gv_ref, qg_ref, qm_ref, qn_ref, kvg_ref, kvm_ref, kvn_ref,
    og_ref, om_ref, on_ref, gug_ref, gum_ref, gun_ref, dg_ref, dm_ref, dn_ref,
):
    rows = a_ref.shape[0]

    def write(grad, momentum, weight, update, outs, index):
        grad = grad.astype(F32)
        outs[0][index] = grad
        outs[1][index] = MOMENTUM_DECAY * momentum[index] + grad
        outs[2][index] = weight[index] - update.astype(F32)

    every = (slice(None), slice(None))
    write(a_ref[:, :QW], mq_ref, wq_ref, sq_ref[0], (qg_ref, qm_ref, qn_ref), every)
    write(a_ref[:, O_AT : O_AT + QW], mo_ref, wo_ref, sq_ref[1], (og_ref, om_ref, on_ref), every)
    write(d_ref[...], md_ref, wd_ref, ud_ref[...], (dg_ref, dm_ref, dn_ref), every)
    for side in range(2):
        index = (slice(None), side, slice(None))
        at = side * O_AT + QW
        write(a_ref[:, at : at + KVW], mkv_ref, wkv_ref, nk_ref[side, :, :KVW], (kvg_ref, kvm_ref, kvn_ref), index)
        write(gu_ref[:, side * FF : side * FF + FF], mgu_ref, wgu_ref, ugu_ref[side], (gug_ref, gum_ref, gun_ref), index)
    gain = jnp.where(
        lane_index(rows) == 0, a_ref[:, HALF:O_AT].astype(F32), a_ref[:, O_AT + HALF :].astype(F32)
    )[:, :2]
    moments = GAIN_DECAY * gainm_ref[...] + gain
    gg_ref[...] = gain
    gm_ref[...] = moments
    gv_ref[...] = gains_ref[...] - gain_rate * moments


def write_outputs(gain_rate, grads, updates, gains, gain_momentum, weights, momenta):
    shapes = [jax.ShapeDtypeStruct(gains.shape, F32)] * 3
    for w in weights:
        shapes += [jax.ShapeDtypeStruct(w.shape, F32)] * 3
    return pl.pallas_call(
        partial(outputs_kernel, gain_rate),
        out_shape=tuple(shapes),
        in_specs=vmem(19),
        out_specs=tuple(vmem(18)),
        compiler_params=pltpu.CompilerParams(vmem_limit_bytes=56 << 20),
        name="outputs",
    )(*grads, *updates, gains, gain_momentum, *weights, *momenta)


def muon_updates(grads, momenta):
    if own_kernels():
        return muon_remote(grads, momenta, lax.axis_size("fsdp"))
    packed, gateup, down = (g.astype(F32) for g in grads)
    m_query, m_keyval, m_out, m_gateup, m_down = momenta

    def moment(momentum, grad):
        return MOMENTUM_DECAY * momentum + grad

    steps = muon_exchange(
        [
            moment(m_query, packed[:, :QW]),
            moment(m_keyval[:, 0], packed[:, QW:HALF]),
            moment(m_keyval[:, 1], packed[:, O_AT + QW : O_AT + HALF]),
            moment(m_out, packed[:, O_AT : O_AT + QW]),
            moment(m_gateup[:, 0], gateup[:, :FF]),
            moment(m_gateup[:, 1], gateup[:, FF:]),
            moment(m_down, down),
        ]
    )
    return (
        jnp.stack([steps[0], steps[3]]).astype(BF16),
        jnp.pad(jnp.stack(steps[1:3]), ((0, 0), (0, 0), (0, NARROW - KVW))).astype(BF16),
        jnp.stack(steps[4:6]).astype(BF16),
        steps[6].astype(BF16),
    )


def local(
    tokens, cotangent, lengths, assignment, norm_gains, gain_momentum, w_query, w_keyval, w_out,
    w_gateup, w_down, m_query, m_keyval, m_out, m_gateup, m_down,
):
    slots = tokens.shape[0] // BLK
    gain_rate = GAIN_SCALE / math.sqrt(assignment.shape[1] * BLK * 3 // 4 * lax.axis_size("fsdp"))
    meta = block_meta(lengths[0], assignment[0], lax.axis_index("dp") * slots, slots)
    inner, outer = rope_constants()
    weights = (w_query, w_keyval, w_out, w_gateup, w_down)
    momenta = (m_query, m_keyval, m_out, m_gateup, m_down)
    packed, gateup, down = gather_weights(weights, norm_gains)
    queries, keyval = project(meta, tokens, packed, inner, outer)
    group_kv = gather_keyval(keyval)
    act, gres, gb, low, gq, dkv, d_gateup, d_down, gain = layer(
        meta, tokens, cotangent, queries, group_kv, packed, gateup, down, inner, outer
    )
    dkv = reduce_keyval(dkv)
    input_grad, d_packed = finish(
        meta, tokens, packed, gq, dkv, gres, gb, low, gain, inner, outer
    )
    grads = reduce_grads((d_packed, d_gateup, d_down))
    updates = muon_updates(grads, momenta)
    return (act, input_grad) + tuple(
        write_outputs(gain_rate, grads, updates, norm_gains, gain_momentum, weights, momenta)
    )


def solution(mesh):
    rows = P(("fsdp", "dp"), None)
    two, three = P("fsdp", None), P("fsdp", None, None)
    return jax.shard_map(
        local,
        mesh=mesh,
        in_specs=(rows, rows, two, two, two, two, two, three, two, three, two, two, three, two, three, two),
        out_specs=(rows, rows) + (two,) * 6 + (three,) * 3 + (two,) * 3 + (three,) * 3 + (two,) * 3,
        check_vma=False,
    )
```

time: 1340 us -> 337 us (0.25)
  waiting for transfers between devices: 417 us -> 0 us
  matrix products: 374 us -> 0 us
  Pallas kernels: 0 us -> 303 us
  blocking collectives: 158 us -> 0 us
  other arithmetic: 132 us -> 4.23 us
  starting transfers between devices: 85.9 us -> 0 us
  local copies, waits for them, and re-layouts: 108 us -> 26.3 us
  loops' own time: 40.6 us -> 0 us
  between operations: 15.8 us -> 1.21 us
    dot_general x72 -> x0, matrix products: 374 us -> none  [the longest x12 86.4 us: block_scores(): jnp.einsum('rhjd,khd->hjrk', queries, kv_block[:, 0], preferred_element_t...]
    pallas_call x0 -> x9, Pallas kernels: none -> 303 us  [the longest x1 71.6 us: layer(): pl.pallas_call(layer_kernel, out_shape=(jax.ShapeDtypeStruct((rows, D), B...]
    unnamed x12 -> x0, waiting for transfers between devices: 237 us -> none
    all_gather x4 -> x0, blocking collectives: 122 us -> none  [the longest x1 34.4 us: local(): lax.all_gather(shard_low[2], 'fsdp', axis=0, tiled=True)]
    all_to_all x2 -> x0, starting transfers between devices: 85.3 us -> none  [the longest x1 79.8 us: local(): lax.all_to_all(for_sending(update_rows), 'fsdp', split_axis=0, concat_axi...]
    reduce_scatter x2 -> x0, waiting for transfers between devices: 82 us -> none  [the longest x1 69.7 us: local(): lax.psum_scatter(local_grads[4].astype(jnp.bfloat16), 'fsdp', scatter_dim...]
    all_to_all x2 -> x0, waiting for transfers between devices: 74.8 us -> none  [the longest x1 40.6 us: local(): lax.all_to_all(outgoing.astype(jnp.bfloat16), 'fsdp', split_axis=0, conca...]
    reduce_sum x11 -> x3, other arithmetic: 55.3 us -> 2.52 us  [the longest x1 0.9 us: block_meta(): jnp.sum(jnp.where(want[:, :, None] == entries[None, None, :], assign_row[...]
  transfers between devices with their start and end apart: 11 -> 0, of which waited for: 8 -> 0; matrix products, arithmetic and copies ran while one was open for 17% -> 0% of each run, Pallas kernels for 0% -> 0%
where the time goes in v1:
time: 337 us; the launch traced here: 335 us
  Pallas kernels  303 us (90%)
  local copies, waits for them, and re-layouts  26.3 us (8%)
  other arithmetic  4.23 us (1%)
    pallas_call x1, Pallas kernels, layer(): pl.pallas_call(layer_kernel, out_shape=(jax.ShapeDtypeStruct((rows, D), B...  71.6 us
    pallas_call x1, Pallas kernels, reduce_grads_remote(): pl.pallas_call(partial(sum_kernel, lines), out_shape=tuple((jax.ShapeDtyp...  62.7 us
    pallas_call x1, Pallas kernels, muon_remote(): pl.pallas_call(partial(muon_kernel, count), out_shape=(jax.ShapeDtypeStru...  55.5 us
    pallas_call x1, Pallas kernels, gather_weights_remote(): pl.pallas_call(partial(gather_kernel, count // 2), out_shape=tuple((jax.S...  50.3 us
    unnamed x65, local copies, waits for them, and re-layouts  25.9 us
    pallas_call x1, Pallas kernels, reduce_keyval_remote(): pl.pallas_call(reduce_keyval_kernel, out_shape=jax.ShapeDtypeStruct((rows...  24.8 us
    pallas_call x1, Pallas kernels, gather_keyval_remote(): pl.pallas_call(gather_keyval_kernel, out_shape=jax.ShapeDtypeStruct((4,)...  19.1 us
    pallas_call x1, Pallas kernels, finish(): pl.pallas_call(finish_kernel, out_shape=(jax.ShapeDtypeStruct((rows, D),...  7.64 us

profile of v1, /device:TPU:0, one launch (start us, length us, event | category | flops | bytes accessed | tf_op | source)
XLA Modules:
  0.0 335.0 jit_solution(8583922097096386464)
XLA Ops:
  0.7 0.9 select_reduce_fusion.1
  3.1 0.7 select_reduce_fusion.2
  4.2 0.9 select_reduce_fusion
  5.3 0.8 copy.58.gains_ref
  6.1 1.2 copy-done.4
  7.3 1.0 copy-done.7
  8.3 0.9 copy-done.14
  9.2 0.9 copy-done.15
  10.1 0.9 copy-done.17
  11.0 50.3 %gather_weights.1 = (bf16[8,72,1792]{2,1,0:T(8,128)(2,1)S(1)}, bf16[8,72,3072]{2,1,0:T(8,128)(2,1)S(1)}, bf16[8,192,576]{2,1,0:T(8,128)(2,1)S(1)}) custom-call(f32[72,576]{1,0:T(8,128)S(1)} %copy-done.14, f32[72,2,192]{2,1,0:T(2,128)S(1)} %copy-done.17, f32[72,576]{1,0:T(8,128)S(1)} %copy-done.15, f32[72,2,1536]{2,1,0:T(2,128)S(1)} %copy-done.4, ...), custom_call_target="tpu_custom_call" | custom-call | tf_op jit(solution)/shard_map/gather_weights/pallas_call | solution.py:753
  61.3 1.8 copy-done.3
  63.1 1.3 copy-done.6
  64.4 2.0 copy.60.x_ref
  66.5 5.8 %project.1 = (bf16[768,1152]{1,0:T(8,128)(2,1)S(1)}, bf16[768,384]{1,0:T(8,128)(2,1)S(1)}) custom-call(s32[6,16]{1,0:T(8,128)S(1)} %concatenate.3.meta, bf16[768,576]{1,0:T(8,128)(2,1)S(1)} %copy.60.x_ref, bf16[576,1792]{1,0:T(8,128)(2,1)S(1)} %bitcast.29, f32[2,128,128]{2,1,0:T(8,128)S(1)} %copy-done.9, f32[2,16,128]{2,1,0:T(8,128)S(1)} %copy-done.19), custom_call_target="tpu_custom_call" | custom-call | tf_op jit(solution)/shard_map/project/pallas_call | solution.py:164
  72.3 1.2 copy-done.8
  73.5 0.8 copy-done.16
  74.3 19.1 %gather_keyval.1 = bf16[4,768,384]{2,1,0:T(8,128)(2,1)} custom-call(bf16[768,384]{1,0:T(8,128)(2,1)} %copy-done.16), custom_call_target="tpu_custom_call" | custom-call | tf_op jit(solution)/shard_map/gather_keyval/pallas_call | solution.py:806
  93.4 1.4 copy.61.cot_ref
  94.8 71.6 %layer.1 = (bf16[768,576]{1,0:T(8,128)(2,1)}, f32[768,576]{1,0:T(8,128)}, bf16[768,640]{1,0:T(8,128)(2,1)}, bf16[768,576]{1,0:T(8,128)(2,1)}, bf16[768,640]{1,0:...) custom-call(s32[6,16]{1,0:T(8,128)} %copy-done.21, ...), custom_call_target="tpu_custom_call" | custom-call | tf_op jit(solution)/shard_map/layer/pallas_call | solution.py:388
  166.4 1.7 copy-done.5
  168.1 24.8 %reduce_keyval.1.dkv_ref = bf16[768,384]{1,0:T(8,128)(2,1)S(1)} custom-call(bf16[4,768,384]{2,1,0:T(8,128)(2,1)S(1)} %bitcast.33), custom_call_target="tpu_custom_call" | custom-call | tf_op jit(solution)/shard_map/reduce_keyval/pallas_call | solution.py:868
  193.1 1.2 copy-done.13
  194.3 0.7 copy-done.23
  195.0 7.6 %finish.1 = (f32[768,576]{1,0:T(8,128)}, bf16[576,1792]{1,0:T(8,128)(2,1)}) custom-call(s32[6,16]{1,0:T(8,128)S(1)} %copy-done.22, bf16[768,576]{1,0:T(8,128)(2,1)S(1)} %copy-done.2, bf16[576,1792]{1,0:T(8,128)(2,1)} %bitcast.31, bf16[768,640]{1,0:T(8,128)(2,1)S(1)} %copy-done.13, bf16[768,384]{1,0:T(8,128)(2,1)S(1)} %reduce_keyval.1.dkv_ref, ...), custom_call_target="tpu_custom_call" | custom-call | tf_op jit(solution)/shard_map/finish/pallas_call | solution.py:471
  202.6 62.7 %sum_grads.1 = (bf16[72,1792]{1,0:T(8,128)(2,1)}, bf16[72,3072]{1,0:T(8,128)(2,1)}, bf16[192,576]{1,0:T(8,128)(2,1)}) custom-call(bf16[8,72,1792]{2,1,0:T(8,128)(2,1)} %bitcast.37, bf16[8,72,3072]{2,1,0:T(8,128)(2,1)} %bitcast.36, bf16[8,192,576]{2,1,0:T(8,128)(2,1)} %bitcast.38), custom_call_target="tpu_custom_call" | custom-call | tf_op jit(solution)/shard_map/sum_grads/pallas_call | solution.py:1040
  265.4 55.5 %muon.1 = (bf16[2,72,576]{2,1,0:T(8,128)(2,1)}, bf16[2,72,256]{2,1,0:T(8,128)(2,1)}, bf16[2,72,1536]{2,1,0:T(8,128)(2,1)}, bf16[192,576]{1,0:T(8,128)(2,1)}) custom-call(bf16[72,1792]{1,0:T(8,128)(2,1)} %get-tuple-element.77.a_ref, bf16[72,3072]{1,0:T(8,128)(2,1)} %get-tuple-element.78.gu_ref, bf16[192,576]{1,0:T(8,128)(2,1)} %get-tuple-element.79.d_ref, ...), custom_call_target="tpu_custom_call" | custom-call | tf_op jit(solution)/shard_map/muon/pallas_call | solution.py:1335
  321.6 5.9 %outputs.1 = (f32[72,2]{1,0:T(8,128)}, f32[72,2]{1,0:T(8,128)}, f32[72,2]{1,0:T(8,128)}, f32[72,576]{1,0:T(8,128)}, f32[72,576]{1,0:T(8,128)}, /*index=5*/f32[72...) custom-call(bf16[72,1792]{1,0:T(8,128)(2,1)} %get-tuple-element.77.a, ...), custom_call_target="tpu_custom_call" | custom-call | tf_op jit(solution)/shard_map/outputs/pallas_call | solution.py:1406
  327.5 1.5 copy.67
  329.0 1.4 copy.68
  330.4 1.4 copy.69
  331.8 1.7 copy.66
  333.5 1.3 copy.65
  (59 shorter events, 2.9 us)
Async XLA Ops:
  0.7 65.8 %copy-start.9 = (f32[2,128,128]{2,1,0:T(8,128)S(1)}, f32[2,128,128]{2,1,0:T(8,128)}, u32[]{:S(2)}) copy-start(f32[2,128,128]{2,1,0:T(8,128)} %constant.51.clone.inner_ref) | copy-start | bytes 393220
  0.7 65.8 %copy-start.19 = (f32[2,16,128]{2,1,0:T(8,128)S(1)}, f32[2,16,128]{2,1,0:T(8,128)}, u32[]{:S(2)}) copy-start(f32[2,16,128]{2,1,0:T(8,128)} %constant.52.clone.outer_ref) | copy-start | bytes 49156
  5.3 66.9 %copy-start.21 = (s32[6,16]{1,0:T(8,128)}, s32[6,16]{1,0:T(8,128)S(1)}, u32[]{:S(2)}) copy-start(s32[6,16]{1,0:T(8,128)S(1)} %concatenate.3.meta) | copy-start | bytes 1156
  6.1 1.2 copy-start.4
  7.3 1.0 copy-start.7
  8.3 0.9 copy-start.14
  9.2 0.9 copy-start.15
  10.1 0.9 copy-start.17
  11.0 61.2 %copy-start.18 = (f32[72,2]{1,0:T(8,128)}, f32[72,2]{1,0:T(8,128)S(1)}, u32[]{:S(2)}) copy-start(f32[72,2]{1,0:T(8,128)S(1)} %copy.58.gains_ref) | copy-start | bytes 1732
  61.3 1.8 copy-start.3
  63.1 1.3 copy-start.6
  64.4 7.9 %copy-start = (bf16[8,72,1792]{2,1,0:T(8,128)(2,1)}, bf16[8,72,1792]{2,1,0:T(8,128)(2,1)S(1)}, u32[]{:S(2)}) copy-start(bf16[8,72,1792]{2,1,0:T(8,128)(2,1)S(1)} %get-tuple-element.61) | copy-start | bytes 6193156
  66.4 27.0 %copy-start.1 = (bf16[768,576]{1,0:T(8,128)(2,1)}, bf16[768,576]{1,0:T(8,128)(2,1)S(1)}, u32[]{:S(2)}) copy-start(bf16[768,576]{1,0:T(8,128)(2,1)S(1)} %copy.60.x_ref) | copy-start | bytes 2654212
  72.3 1.2 copy-start.8
  73.5 0.8 copy-start.16
  74.3 19.1 %copy-start.26 = (bf16[768,576]{0,1:T(8,128)(2,1)S(1)}, bf16[768,576]{0,1:T(8,128)(2,1)}, u32[]{:S(2)}) copy-start(bf16[768,576]{0,1:T(8,128)(2,1)} %param.19) | copy-start | bytes 2654212
  94.8 98.2 %copy-start.10 = (f32[2,128,128]{2,1,0:T(8,128)S(1)}, f32[2,128,128]{2,1,0:T(8,128)}, u32[]{:S(2)}) copy-start(f32[2,128,128]{2,1,0:T(8,128)} %constant.51.clone.inner_ref) | copy-start | bytes 393220
  94.8 98.2 %copy-start.20 = (f32[2,16,128]{2,1,0:T(8,128)S(1)}, f32[2,16,128]{2,1,0:T(8,128)}, u32[]{:S(2)}) copy-start(f32[2,16,128]{2,1,0:T(8,128)} %constant.52.clone.outer_ref) | copy-start | bytes 49156
  94.8 98.2 %copy-start.22 = (s32[6,16]{1,0:T(8,128)S(1)}, s32[6,16]{1,0:T(8,128)}, u32[]{:S(2)}) copy-start(s32[6,16]{1,0:T(8,128)} %copy-done.21) | copy-start | bytes 1156
  166.4 26.6 %copy-start.2 = (bf16[768,576]{1,0:T(8,128)(2,1)S(1)}, bf16[768,576]{1,0:T(8,128)(2,1)}, u32[]{:S(2)}) copy-start(bf16[768,576]{1,0:T(8,128)(2,1)} %copy-done.1) | copy-start | bytes 2654212
  166.4 1.8 copy-start.5
  168.1 24.9 %copy-start.11 = (bf16[768,640]{1,0:T(8,128)(2,1)S(1)}, bf16[768,640]{1,0:T(8,128)(2,1)}, u32[]{:S(2)}) copy-start(bf16[768,640]{1,0:T(8,128)(2,1)} %get-tuple-element.70.gb_ref) | copy-start | bytes 2949124
  168.1 24.9 %copy-start.12 = (bf16[768,576]{1,0:T(8,128)(2,1)S(1)}, bf16[768,576]{1,0:T(8,128)(2,1)}, u32[]{:S(2)}) copy-start(bf16[768,576]{1,0:T(8,128)(2,1)} %get-tuple-element.71.low_ref) | copy-start | bytes 2654212
  193.0 1.2 copy-start.13
  194.2 0.7 copy-start.23
  265.3 55.5 %copy-start.27 = (f32[72,2]{0,1:T(2,128)S(1)}, f32[72,2]{0,1:T(2,128)}, u32[]{:S(2)}) copy-start(f32[72,2]{0,1:T(2,128)} %param.23) | copy-start | bytes 1732
  321.6 10.2 %copy-start.24 = (f32[768,576]{1,0:T(8,128)S(1)}, f32[768,576]{1,0:T(8,128)}, u32[]{:S(2)}) copy-start(f32[768,576]{1,0:T(8,128)} %get-tuple-element.123) | copy-start | bytes 5308420
  327.5 6.0 %copy-start.25 = (bf16[768,576]{1,0:T(8,128)(2,1)S(1)}, bf16[768,576]{1,0:T(8,128)(2,1)}, u32[]{:S(2)}) copy-start(bf16[768,576]{1,0:T(8,128)(2,1)} %get-tuple-element.122) | copy-start | bytes 2654212
